TPU v7x, 32 devices: a whole 2x2x4 slice. The times are simulated.
32 devices in a mesh: segment: 4 (over z), space: 8 (over y, x, core).
Axes of the slice: x: 2, y: 2, z: 4, core: 2. Of those that a mesh axis runs over, the one named last changes fastest.
Arguments:
- video: bfloat16 [4, 2, 32, 24, 256], P(None, None, 'space'), may hold values from -6 to 6
- spatial_weight: bfloat16 [4, 2, 2, 2304, 256], P('segment'), may hold values from -0.125 to 0.125
- temporal_weight: bfloat16 [4, 2, 2, 768, 256], P('segment'), may hold values from -0.21875 to 0.21875
- section_blocks: int32 [4], P('segment'), may hold values from 1 to 2, as said below
Outputs:
- section_out: bfloat16 [4, 4, 2, 32, 24, 256], P('segment', None, None, 'space')
Inputs may be any that keep to these rules, and one draw needn't show every extreme that they name: `section_blocks`: some section runs 2 blocks.
All inputs are finite; a program needn't handle non-finite values.
Results may differ from a plain program's by a relative error of at most 0.038.
Values may be sent and summed in bfloat16 or wider, within the bound.
A program may use at most 64 MiB of HBM per device.

v0:
```python
import jax
import jax.numpy as jnp
from jax import lax
from jax.sharding import PartitionSpec as P


def with_halo(block, sides, width):
    for axis, dim in sides:
        count = lax.axis_size(axis)
        forward = [(i, i + 1) for i in range(count - 1)]
        backward = [(target, source) for source, target in forward]
        low = lax.ppermute(
            lax.slice_in_dim(block, block.shape[dim] - width, None, axis=dim), axis, forward
        )
        high = lax.ppermute(lax.slice_in_dim(block, 0, width, axis=dim), axis, backward)
        block = jnp.concatenate([low, block, high], axis=dim)
    return block


def from_behind(value, axis, steps):
    count = lax.axis_size(axis)
    initial, last = (max(0, -steps), min(count, count - steps))
    return lax.ppermute(value, axis, [(source, source + steps) for source in range(initial, last)])


def pad_columns(active):
    return jnp.pad(active, ((0, 0), (0, 0), (1, 1), (0, 0)))


def tap_sum(padded, weight, rows_used, offset, count):
    channels = padded.shape[-1]
    columns = padded.shape[2] - 2
    pieces = [
        padded[:, row_tap - offset : row_tap - offset + count, col_tap : col_tap + columns]
        for row_tap in rows_used
        for col_tap in range(3)
    ]
    stacked = jnp.concatenate(pieces, -1)
    kernel = jnp.concatenate(
        [weight[3 * row_tap * channels : (3 * row_tap + 3) * channels] for row_tap in rows_used], 0
    )
    summed = jnp.dot(
        stacked.reshape(-1, stacked.shape[-1]), kernel, preferred_element_type=jnp.float32
    )
    return summed.reshape(padded.shape[0], count, columns, channels)


def fetch_rims(active):
    return with_halo(active, (("space", 1),), 1)


def conv_rows(active, weight):
    rows = active.shape[1]
    return tap_sum(pad_columns(fetch_rims(active)), weight, (0, 1, 2), 0, rows)


def temporal_step(spatial_out, cache, opening, weight):
    frames = spatial_out.shape[0]
    starting = jnp.broadcast_to(spatial_out[:1], cache.shape)
    earlier = jnp.where(opening, starting, cache)
    joined = jnp.concatenate([earlier, spatial_out], 0)
    stacked = jnp.concatenate(
        [joined[0:frames], joined[1 : frames + 1], joined[2 : frames + 2]], -1
    )
    mixed = jnp.dot(
        stacked.reshape(-1, stacked.shape[-1]), weight, preferred_element_type=jnp.float32
    )
    return (mixed.reshape(spatial_out.shape), joined[frames:])


def block_plain(state, caches, opening, spatial_pair, temporal_pair):
    active = jax.nn.silu(state.astype(jnp.float32)).astype(jnp.bfloat16)
    first_out = conv_rows(active, spatial_pair[0]).astype(jnp.bfloat16)
    mixed, cache_one = temporal_step(first_out, caches[0], opening, temporal_pair[0])
    hidden = jax.nn.silu(mixed).astype(jnp.bfloat16)
    second_out = conv_rows(hidden, spatial_pair[1]).astype(jnp.bfloat16)
    mixed_two, cache_two = temporal_step(second_out, caches[1], opening, temporal_pair[1])
    return ((state.astype(jnp.float32) + mixed_two).astype(jnp.bfloat16), (cache_one, cache_two))


def per_device(video, spatial_weight, temporal_weight, section_blocks):
    micro = video.shape[0]
    frames, rows, columns, channels = video.shape[1:]
    segments = lax.axis_size("segment")
    place = lax.axis_index("segment")
    depth = section_blocks[0]
    spatial_set = spatial_weight[0]
    temporal_set = temporal_weight[0]
    blocks = spatial_set.shape[0]
    margin = 0
    caches = tuple(
        (
            (
                jnp.zeros((2, rows + margin, columns, channels), jnp.bfloat16),
                jnp.zeros((2, rows, columns, channels), jnp.bfloat16),
            )
            for block_index in range(blocks)
        )
    )
    outputs = jnp.zeros(video.shape, jnp.bfloat16)
    incoming = jnp.zeros(video.shape[1:], jnp.bfloat16)

    def advance(step_index, carry):
        arrived, held, stored = carry
        group = step_index - place
        live = (group >= 0) & (group < micro)
        slot = jnp.clip(group, 0, micro - 1)
        loaded = lax.dynamic_index_in_dim(video, slot, 0, keepdims=False)
        state = jnp.where(place == 0, loaded, arrived)
        opening = group == 0
        renewed = []
        for block_index in range(blocks):
            result, fresh = block_plain(
                state,
                held[block_index],
                opening,
                spatial_set[block_index],
                temporal_set[block_index],
            )
            active_block = block_index < depth
            state = jnp.where(active_block, result, state)
            keeping = live & active_block
            renewed.append(
                (
                    jnp.where(keeping, fresh[0], held[block_index][0]),
                    jnp.where(keeping, fresh[1], held[block_index][1]),
                )
            )
        previous = lax.dynamic_index_in_dim(stored, slot, 0, keepdims=False)
        stored = lax.dynamic_update_index_in_dim(stored, jnp.where(live, state, previous), slot, 0)
        passed = from_behind(state, "segment", 1)
        return (passed, tuple(renewed), stored)

    final = lax.fori_loop(0, micro + segments - 1, advance, (incoming, caches, outputs))
    return final[2][None]


def solution(mesh):
    return jax.shard_map(
        per_device,
        mesh=mesh,
        in_specs=(
            P(None, None, "space", None, None),
            P("segment", None, None, None, None),
            P("segment", None, None, None, None),
            P("segment"),
        ),
        out_specs=P("segment", None, None, "space", None, None),
        check_vma=False,
    )
```

profile of v0, /device:TPU:27, one launch (start us, length us, event | category | flops | bytes accessed | tf_op | source)
XLA Modules:
  0.0 331.3 jit_solution(5974494817458108186)
XLA Ops:
  5.1 325.5 %while.26 = (s32[]{:T(128)}, bf16[2,4,24,256]{3,2,1,0:T(8,128)(2,1)S(1)}, bf16[2,4,24,256]{3,2,1,0:T(8,128)(2,1)S(1)}, bf16[2,4,24,256]{3,2,1,0:T(8,128)(2,1)S(1...) while((s32[]{:T(128)}, ...), condition=%wide.region_1.2_spmd.clone, body=%wide.region_0.1_spmd.clone.sunk | while | flops 1220788224 | bytes 46744328 | solution.py:134
  17.9 4.8 %collective-permute-start.3 = (bf16[2,1,24,256]{3,2,1,0:T(8,128)(2,1)S(1)}, bf16[2,1,24,256]{3,2,1,0:T(8,128)(2,1)S(1)}, u32[]{:S(2)}, u32[]{:S(2)}) collective-permute-start(bf16[2,1,24,256]{3,2,1,0:T(8,128)(2,1)S(1)} %get-tuple-element.573), channel_id=1, source_target_pairs={{0,1},{1,2},{2,3},{3,4},{4,5},{5,6},{6,7},{8,9},{9,10},{10,11},{11... | collective-permute-start | bytes 73736 | tf_op jit(solution)/shard_map/while/body/eval_jaxpr/ppermute | solution.py:12
  27.6 5.1 %collective-permute-start.5 = (bf16[2,1,24,256]{3,2,1,0:T(8,128)(2,1)S(1)}, bf16[2,1,24,256]{3,2,1,0:T(8,128)(2,1)S(1)}, u32[]{:S(2)}, u32[]{:S(2)}) collective-permute-start(bf16[2,1,24,256]{3,2,1,0:T(8,128)(2,1)S(1)} %get-tuple-element.578), channel_id=1, source_target_pairs={{0,1},{1,2},{2,3},{3,4},{4,5},{5,6},{6,7},{8,9},{9,10},{10,11},{11... | collective-permute-start | bytes 73736 | tf_op jit(solution)/shard_map/while/body/eval_jaxpr/ppermute | solution.py:12
  37.6 5.1 %collective-permute-start.7 = (bf16[2,1,24,256]{3,2,1,0:T(8,128)(2,1)S(1)}, bf16[2,1,24,256]{3,2,1,0:T(8,128)(2,1)S(1)}, u32[]{:S(2)}, u32[]{:S(2)}) collective-permute-start(bf16[2,1,24,256]{3,2,1,0:T(8,128)(2,1)S(1)} %get-tuple-element.581), channel_id=1, source_target_pairs={{0,1},{1,2},{2,3},{3,4},{4,5},{5,6},{6,7},{8,9},{9,10},{10,11},{11... | collective-permute-start | bytes 73736 | tf_op jit(solution)/shard_map/while/body/eval_jaxpr/ppermute | solution.py:12
  53.1 6.3 %collective-permute-start.1 = (bf16[2,1,24,256]{3,2,1,0:T(8,128)(2,1)S(1)}, bf16[2,1,24,256]{3,2,1,0:T(8,128)(2,1)S(1)}, u32[]{:S(2)}, u32[]{:S(2)}) collective-permute-start(bf16[2,1,24,256]{3,2,1,0:T(8,128)(2,1)S(1)} %get-tuple-element.570), channel_id=1, source_target_pairs={{0,1},{1,2},{2,3},{3,4},{4,5},{5,6},{6,7},{8,9},{9,10},{10,11},{11... | collective-permute-start | bytes 73736 | tf_op jit(solution)/shard_map/while/body/eval_jaxpr/ppermute | solution.py:12
  64.4 5.0 %collective-permute-start.3 = (bf16[2,1,24,256]{3,2,1,0:T(8,128)(2,1)S(1)}, bf16[2,1,24,256]{3,2,1,0:T(8,128)(2,1)S(1)}, u32[]{:S(2)}, u32[]{:S(2)}) collective-permute-start(bf16[2,1,24,256]{3,2,1,0:T(8,128)(2,1)S(1)} %get-tuple-element.573), channel_id=1, source_target_pairs={{0,1},{1,2},{2,3},{3,4},{4,5},{5,6},{6,7},{8,9},{9,10},{10,11},{11... | collective-permute-start | bytes 73736 | tf_op jit(solution)/shard_map/while/body/eval_jaxpr/ppermute | solution.py:12
  74.4 5.1 %collective-permute-start.5 = (bf16[2,1,24,256]{3,2,1,0:T(8,128)(2,1)S(1)}, bf16[2,1,24,256]{3,2,1,0:T(8,128)(2,1)S(1)}, u32[]{:S(2)}, u32[]{:S(2)}) collective-permute-start(bf16[2,1,24,256]{3,2,1,0:T(8,128)(2,1)S(1)} %get-tuple-element.578), channel_id=1, source_target_pairs={{0,1},{1,2},{2,3},{3,4},{4,5},{5,6},{6,7},{8,9},{9,10},{10,11},{11... | collective-permute-start | bytes 73736 | tf_op jit(solution)/shard_map/while/body/eval_jaxpr/ppermute | solution.py:12
  84.4 5.1 %collective-permute-start.7 = (bf16[2,1,24,256]{3,2,1,0:T(8,128)(2,1)S(1)}, bf16[2,1,24,256]{3,2,1,0:T(8,128)(2,1)S(1)}, u32[]{:S(2)}, u32[]{:S(2)}) collective-permute-start(bf16[2,1,24,256]{3,2,1,0:T(8,128)(2,1)S(1)} %get-tuple-element.581), channel_id=1, source_target_pairs={{0,1},{1,2},{2,3},{3,4},{4,5},{5,6},{6,7},{8,9},{9,10},{10,11},{11... | collective-permute-start | bytes 73736 | tf_op jit(solution)/shard_map/while/body/eval_jaxpr/ppermute | solution.py:12
  99.8 6.3 %collective-permute-start.1 = (bf16[2,1,24,256]{3,2,1,0:T(8,128)(2,1)S(1)}, bf16[2,1,24,256]{3,2,1,0:T(8,128)(2,1)S(1)}, u32[]{:S(2)}, u32[]{:S(2)}) collective-permute-start(bf16[2,1,24,256]{3,2,1,0:T(8,128)(2,1)S(1)} %get-tuple-element.570), channel_id=1, source_target_pairs={{0,1},{1,2},{2,3},{3,4},{4,5},{5,6},{6,7},{8,9},{9,10},{10,11},{11... | collective-permute-start | bytes 73736 | tf_op jit(solution)/shard_map/while/body/eval_jaxpr/ppermute | solution.py:12
  111.1 5.0 %collective-permute-start.3 = (bf16[2,1,24,256]{3,2,1,0:T(8,128)(2,1)S(1)}, bf16[2,1,24,256]{3,2,1,0:T(8,128)(2,1)S(1)}, u32[]{:S(2)}, u32[]{:S(2)}) collective-permute-start(bf16[2,1,24,256]{3,2,1,0:T(8,128)(2,1)S(1)} %get-tuple-element.573), channel_id=1, source_target_pairs={{0,1},{1,2},{2,3},{3,4},{4,5},{5,6},{6,7},{8,9},{9,10},{10,11},{11... | collective-permute-start | bytes 73736 | tf_op jit(solution)/shard_map/while/body/eval_jaxpr/ppermute | solution.py:12
  121.1 5.1 %collective-permute-start.5 = (bf16[2,1,24,256]{3,2,1,0:T(8,128)(2,1)S(1)}, bf16[2,1,24,256]{3,2,1,0:T(8,128)(2,1)S(1)}, u32[]{:S(2)}, u32[]{:S(2)}) collective-permute-start(bf16[2,1,24,256]{3,2,1,0:T(8,128)(2,1)S(1)} %get-tuple-element.578), channel_id=1, source_target_pairs={{0,1},{1,2},{2,3},{3,4},{4,5},{5,6},{6,7},{8,9},{9,10},{10,11},{11... | collective-permute-start | bytes 73736 | tf_op jit(solution)/shard_map/while/body/eval_jaxpr/ppermute | solution.py:12
  131.1 5.1 %collective-permute-start.7 = (bf16[2,1,24,256]{3,2,1,0:T(8,128)(2,1)S(1)}, bf16[2,1,24,256]{3,2,1,0:T(8,128)(2,1)S(1)}, u32[]{:S(2)}, u32[]{:S(2)}) collective-permute-start(bf16[2,1,24,256]{3,2,1,0:T(8,128)(2,1)S(1)} %get-tuple-element.581), channel_id=1, source_target_pairs={{0,1},{1,2},{2,3},{3,4},{4,5},{5,6},{6,7},{8,9},{9,10},{10,11},{11... | collective-permute-start | bytes 73736 | tf_op jit(solution)/shard_map/while/body/eval_jaxpr/ppermute | solution.py:12
  139.6 4.1 %collective-permute-done.8 = bf16[2,4,24,256]{3,2,1,0:T(8,128)(2,1)S(1)} collective-permute-done((bf16[2,4,24,256]{3,2,1,0:T(8,128)(2,1)S(1)}, bf16[2,4,24,256]{3,2,1,0:T(8,128)(2,1)S(1)}, u32[]{:S(2)}, u32[]{:S(2)}) %collective-permute-start.8) | collective-permute-done | bytes 98336 | tf_op jit(solution)/shard_map/while/body/eval_jaxpr/ppermute | solution.py:23
  146.5 6.3 %collective-permute-start.1 = (bf16[2,1,24,256]{3,2,1,0:T(8,128)(2,1)S(1)}, bf16[2,1,24,256]{3,2,1,0:T(8,128)(2,1)S(1)}, u32[]{:S(2)}, u32[]{:S(2)}) collective-permute-start(bf16[2,1,24,256]{3,2,1,0:T(8,128)(2,1)S(1)} %get-tuple-element.570), channel_id=1, source_target_pairs={{0,1},{1,2},{2,3},{3,4},{4,5},{5,6},{6,7},{8,9},{9,10},{10,11},{11... | collective-permute-start | bytes 73736 | tf_op jit(solution)/shard_map/while/body/eval_jaxpr/ppermute | solution.py:12
  157.9 5.0 %collective-permute-start.3 = (bf16[2,1,24,256]{3,2,1,0:T(8,128)(2,1)S(1)}, bf16[2,1,24,256]{3,2,1,0:T(8,128)(2,1)S(1)}, u32[]{:S(2)}, u32[]{:S(2)}) collective-permute-start(bf16[2,1,24,256]{3,2,1,0:T(8,128)(2,1)S(1)} %get-tuple-element.573), channel_id=1, source_target_pairs={{0,1},{1,2},{2,3},{3,4},{4,5},{5,6},{6,7},{8,9},{9,10},{10,11},{11... | collective-permute-start | bytes 73736 | tf_op jit(solution)/shard_map/while/body/eval_jaxpr/ppermute | solution.py:12
  167.8 5.1 %collective-permute-start.5 = (bf16[2,1,24,256]{3,2,1,0:T(8,128)(2,1)S(1)}, bf16[2,1,24,256]{3,2,1,0:T(8,128)(2,1)S(1)}, u32[]{:S(2)}, u32[]{:S(2)}) collective-permute-start(bf16[2,1,24,256]{3,2,1,0:T(8,128)(2,1)S(1)} %get-tuple-element.578), channel_id=1, source_target_pairs={{0,1},{1,2},{2,3},{3,4},{4,5},{5,6},{6,7},{8,9},{9,10},{10,11},{11... | collective-permute-start | bytes 73736 | tf_op jit(solution)/shard_map/while/body/eval_jaxpr/ppermute | solution.py:12
  177.9 5.1 %collective-permute-start.7 = (bf16[2,1,24,256]{3,2,1,0:T(8,128)(2,1)S(1)}, bf16[2,1,24,256]{3,2,1,0:T(8,128)(2,1)S(1)}, u32[]{:S(2)}, u32[]{:S(2)}) collective-permute-start(bf16[2,1,24,256]{3,2,1,0:T(8,128)(2,1)S(1)} %get-tuple-element.581), channel_id=1, source_target_pairs={{0,1},{1,2},{2,3},{3,4},{4,5},{5,6},{6,7},{8,9},{9,10},{10,11},{11... | collective-permute-start | bytes 73736 | tf_op jit(solution)/shard_map/while/body/eval_jaxpr/ppermute | solution.py:12
  186.3 4.1 %collective-permute-done.8 = bf16[2,4,24,256]{3,2,1,0:T(8,128)(2,1)S(1)} collective-permute-done((bf16[2,4,24,256]{3,2,1,0:T(8,128)(2,1)S(1)}, bf16[2,4,24,256]{3,2,1,0:T(8,128)(2,1)S(1)}, u32[]{:S(2)}, u32[]{:S(2)}) %collective-permute-start.8) | collective-permute-done | bytes 98336 | tf_op jit(solution)/shard_map/while/body/eval_jaxpr/ppermute | solution.py:23
  193.3 6.3 %collective-permute-start.1 = (bf16[2,1,24,256]{3,2,1,0:T(8,128)(2,1)S(1)}, bf16[2,1,24,256]{3,2,1,0:T(8,128)(2,1)S(1)}, u32[]{:S(2)}, u32[]{:S(2)}) collective-permute-start(bf16[2,1,24,256]{3,2,1,0:T(8,128)(2,1)S(1)} %get-tuple-element.570), channel_id=1, source_target_pairs={{0,1},{1,2},{2,3},{3,4},{4,5},{5,6},{6,7},{8,9},{9,10},{10,11},{11... | collective-permute-start | bytes 73736 | tf_op jit(solution)/shard_map/while/body/eval_jaxpr/ppermute | solution.py:12
  204.6 5.0 %collective-permute-start.3 = (bf16[2,1,24,256]{3,2,1,0:T(8,128)(2,1)S(1)}, bf16[2,1,24,256]{3,2,1,0:T(8,128)(2,1)S(1)}, u32[]{:S(2)}, u32[]{:S(2)}) collective-permute-start(bf16[2,1,24,256]{3,2,1,0:T(8,128)(2,1)S(1)} %get-tuple-element.573), channel_id=1, source_target_pairs={{0,1},{1,2},{2,3},{3,4},{4,5},{5,6},{6,7},{8,9},{9,10},{10,11},{11... | collective-permute-start | bytes 73736 | tf_op jit(solution)/shard_map/while/body/eval_jaxpr/ppermute | solution.py:12
  214.6 5.1 %collective-permute-start.5 = (bf16[2,1,24,256]{3,2,1,0:T(8,128)(2,1)S(1)}, bf16[2,1,24,256]{3,2,1,0:T(8,128)(2,1)S(1)}, u32[]{:S(2)}, u32[]{:S(2)}) collective-permute-start(bf16[2,1,24,256]{3,2,1,0:T(8,128)(2,1)S(1)} %get-tuple-element.578), channel_id=1, source_target_pairs={{0,1},{1,2},{2,3},{3,4},{4,5},{5,6},{6,7},{8,9},{9,10},{10,11},{11... | collective-permute-start | bytes 73736 | tf_op jit(solution)/shard_map/while/body/eval_jaxpr/ppermute | solution.py:12
  224.6 5.1 %collective-permute-start.7 = (bf16[2,1,24,256]{3,2,1,0:T(8,128)(2,1)S(1)}, bf16[2,1,24,256]{3,2,1,0:T(8,128)(2,1)S(1)}, u32[]{:S(2)}, u32[]{:S(2)}) collective-permute-start(bf16[2,1,24,256]{3,2,1,0:T(8,128)(2,1)S(1)} %get-tuple-element.581), channel_id=1, source_target_pairs={{0,1},{1,2},{2,3},{3,4},{4,5},{5,6},{6,7},{8,9},{9,10},{10,11},{11... | collective-permute-start | bytes 73736 | tf_op jit(solution)/shard_map/while/body/eval_jaxpr/ppermute | solution.py:12
  233.1 4.1 %collective-permute-done.8 = bf16[2,4,24,256]{3,2,1,0:T(8,128)(2,1)S(1)} collective-permute-done((bf16[2,4,24,256]{3,2,1,0:T(8,128)(2,1)S(1)}, bf16[2,4,24,256]{3,2,1,0:T(8,128)(2,1)S(1)}, u32[]{:S(2)}, u32[]{:S(2)}) %collective-permute-start.8) | collective-permute-done | bytes 98336 | tf_op jit(solution)/shard_map/while/body/eval_jaxpr/ppermute | solution.py:23
  240.0 6.3 %collective-permute-start.1 = (bf16[2,1,24,256]{3,2,1,0:T(8,128)(2,1)S(1)}, bf16[2,1,24,256]{3,2,1,0:T(8,128)(2,1)S(1)}, u32[]{:S(2)}, u32[]{:S(2)}) collective-permute-start(bf16[2,1,24,256]{3,2,1,0:T(8,128)(2,1)S(1)} %get-tuple-element.570), channel_id=1, source_target_pairs={{0,1},{1,2},{2,3},{3,4},{4,5},{5,6},{6,7},{8,9},{9,10},{10,11},{11... | collective-permute-start | bytes 73736 | tf_op jit(solution)/shard_map/while/body/eval_jaxpr/ppermute | solution.py:12
  251.4 5.0 %collective-permute-start.3 = (bf16[2,1,24,256]{3,2,1,0:T(8,128)(2,1)S(1)}, bf16[2,1,24,256]{3,2,1,0:T(8,128)(2,1)S(1)}, u32[]{:S(2)}, u32[]{:S(2)}) collective-permute-start(bf16[2,1,24,256]{3,2,1,0:T(8,128)(2,1)S(1)} %get-tuple-element.573), channel_id=1, source_target_pairs={{0,1},{1,2},{2,3},{3,4},{4,5},{5,6},{6,7},{8,9},{9,10},{10,11},{11... | collective-permute-start | bytes 73736 | tf_op jit(solution)/shard_map/while/body/eval_jaxpr/ppermute | solution.py:12
  261.3 5.1 %collective-permute-start.5 = (bf16[2,1,24,256]{3,2,1,0:T(8,128)(2,1)S(1)}, bf16[2,1,24,256]{3,2,1,0:T(8,128)(2,1)S(1)}, u32[]{:S(2)}, u32[]{:S(2)}) collective-permute-start(bf16[2,1,24,256]{3,2,1,0:T(8,128)(2,1)S(1)} %get-tuple-element.578), channel_id=1, source_target_pairs={{0,1},{1,2},{2,3},{3,4},{4,5},{5,6},{6,7},{8,9},{9,10},{10,11},{11... | collective-permute-start | bytes 73736 | tf_op jit(solution)/shard_map/while/body/eval_jaxpr/ppermute | solution.py:12
  271.3 5.1 %collective-permute-start.7 = (bf16[2,1,24,256]{3,2,1,0:T(8,128)(2,1)S(1)}, bf16[2,1,24,256]{3,2,1,0:T(8,128)(2,1)S(1)}, u32[]{:S(2)}, u32[]{:S(2)}) collective-permute-start(bf16[2,1,24,256]{3,2,1,0:T(8,128)(2,1)S(1)} %get-tuple-element.581), channel_id=1, source_target_pairs={{0,1},{1,2},{2,3},{3,4},{4,5},{5,6},{6,7},{8,9},{9,10},{10,11},{11... | collective-permute-start | bytes 73736 | tf_op jit(solution)/shard_map/while/body/eval_jaxpr/ppermute | solution.py:12
  279.8 4.1 %collective-permute-done.8 = bf16[2,4,24,256]{3,2,1,0:T(8,128)(2,1)S(1)} collective-permute-done((bf16[2,4,24,256]{3,2,1,0:T(8,128)(2,1)S(1)}, bf16[2,4,24,256]{3,2,1,0:T(8,128)(2,1)S(1)}, u32[]{:S(2)}, u32[]{:S(2)}) %collective-permute-start.8) | collective-permute-done | bytes 98336 | tf_op jit(solution)/shard_map/while/body/eval_jaxpr/ppermute | solution.py:23
  286.8 6.3 %collective-permute-start.1 = (bf16[2,1,24,256]{3,2,1,0:T(8,128)(2,1)S(1)}, bf16[2,1,24,256]{3,2,1,0:T(8,128)(2,1)S(1)}, u32[]{:S(2)}, u32[]{:S(2)}) collective-permute-start(bf16[2,1,24,256]{3,2,1,0:T(8,128)(2,1)S(1)} %get-tuple-element.570), channel_id=1, source_target_pairs={{0,1},{1,2},{2,3},{3,4},{4,5},{5,6},{6,7},{8,9},{9,10},{10,11},{11... | collective-permute-start | bytes 73736 | tf_op jit(solution)/shard_map/while/body/eval_jaxpr/ppermute | solution.py:12
  298.1 5.0 %collective-permute-start.3 = (bf16[2,1,24,256]{3,2,1,0:T(8,128)(2,1)S(1)}, bf16[2,1,24,256]{3,2,1,0:T(8,128)(2,1)S(1)}, u32[]{:S(2)}, u32[]{:S(2)}) collective-permute-start(bf16[2,1,24,256]{3,2,1,0:T(8,128)(2,1)S(1)} %get-tuple-element.573), channel_id=1, source_target_pairs={{0,1},{1,2},{2,3},{3,4},{4,5},{5,6},{6,7},{8,9},{9,10},{10,11},{11... | collective-permute-start | bytes 73736 | tf_op jit(solution)/shard_map/while/body/eval_jaxpr/ppermute | solution.py:12
  308.0 5.1 %collective-permute-start.5 = (bf16[2,1,24,256]{3,2,1,0:T(8,128)(2,1)S(1)}, bf16[2,1,24,256]{3,2,1,0:T(8,128)(2,1)S(1)}, u32[]{:S(2)}, u32[]{:S(2)}) collective-permute-start(bf16[2,1,24,256]{3,2,1,0:T(8,128)(2,1)S(1)} %get-tuple-element.578), channel_id=1, source_target_pairs={{0,1},{1,2},{2,3},{3,4},{4,5},{5,6},{6,7},{8,9},{9,10},{10,11},{11... | collective-permute-start | bytes 73736 | tf_op jit(solution)/shard_map/while/body/eval_jaxpr/ppermute | solution.py:12
  318.1 5.1 %collective-permute-start.7 = (bf16[2,1,24,256]{3,2,1,0:T(8,128)(2,1)S(1)}, bf16[2,1,24,256]{3,2,1,0:T(8,128)(2,1)S(1)}, u32[]{:S(2)}, u32[]{:S(2)}) collective-permute-start(bf16[2,1,24,256]{3,2,1,0:T(8,128)(2,1)S(1)} %get-tuple-element.581), channel_id=1, source_target_pairs={{0,1},{1,2},{2,3},{3,4},{4,5},{5,6},{6,7},{8,9},{9,10},{10,11},{11... | collective-permute-start | bytes 73736 | tf_op jit(solution)/shard_map/while/body/eval_jaxpr/ppermute | solution.py:12
  (596 shorter events, 165.7 us)
Async XLA Ops:
  15.6 7.1 %collective-permute-start.2 = (bf16[2,1,24,256]{3,2,1,0:T(8,128)(2,1)S(1)}, bf16[2,1,24,256]{3,2,1,0:T(8,128)(2,1)S(1)}, u32[]{:S(2)}, u32[]{:S(2)}) collective-permute-start(bf16[2,1,24,256]{3,2,1,0:T(8,128)(2,1)S(1)} %get-tuple-element.572), channel_id=1, source_target_pairs={{1,0},{2,1},{3,2},{4,3},{5,4},{6,5},{7,6},{9,8},{10,9},{11,10},{12... | collective-permute-start | bytes 73736 | tf_op jit(solution)/shard_map/while/body/eval_jaxpr/ppermute | solution.py:15
  25.7 7.1 %collective-permute-start.4 = (bf16[2,1,24,256]{3,2,1,0:T(8,128)(2,1)S(1)}, bf16[2,1,24,256]{3,2,1,0:T(8,128)(2,1)S(1)}, u32[]{:S(2)}, u32[]{:S(2)}) collective-permute-start(bf16[2,1,24,256]{3,2,1,0:T(8,128)(2,1)S(1)} %get-tuple-element.577), channel_id=1, source_target_pairs={{1,0},{2,1},{3,2},{4,3},{5,4},{6,5},{7,6},{9,8},{10,9},{11,10},{12... | collective-permute-start | bytes 73736 | tf_op jit(solution)/shard_map/while/body/eval_jaxpr/ppermute | solution.py:15
  35.7 7.1 %collective-permute-start.6 = (bf16[2,1,24,256]{3,2,1,0:T(8,128)(2,1)S(1)}, bf16[2,1,24,256]{3,2,1,0:T(8,128)(2,1)S(1)}, u32[]{:S(2)}, u32[]{:S(2)}) collective-permute-start(bf16[2,1,24,256]{3,2,1,0:T(8,128)(2,1)S(1)} %get-tuple-element.580), channel_id=1, source_target_pairs={{1,0},{2,1},{3,2},{4,3},{5,4},{6,5},{7,6},{9,8},{10,9},{11,10},{12... | collective-permute-start | bytes 73736 | tf_op jit(solution)/shard_map/while/body/eval_jaxpr/ppermute | solution.py:15
  51.1 8.2 %collective-permute-start = (bf16[2,1,24,256]{3,2,1,0:T(8,128)(2,1)S(1)}, bf16[2,1,24,256]{3,2,1,0:T(8,128)(2,1)S(1)}, u32[]{:S(2)}, u32[]{:S(2)}) collective-permute-start(bf16[2,1,24,256]{3,2,1,0:T(8,128)(2,1)S(1)} %get-tuple-element.569), channel_id=1, source_target_pairs={{1,0},{2,1},{3,2},{4,3},{5,4},{6,5},{7,6},{9,8},{10,9},{11,10},{12... | collective-permute-start | bytes 73736 | tf_op jit(solution)/shard_map/while/body/eval_jaxpr/ppermute | solution.py:15
  53.1 7.2 %collective-permute-start.1 = (bf16[2,1,24,256]{3,2,1,0:T(8,128)(2,1)S(1)}, bf16[2,1,24,256]{3,2,1,0:T(8,128)(2,1)S(1)}, u32[]{:S(2)}, u32[]{:S(2)}) collective-permute-start(bf16[2,1,24,256]{3,2,1,0:T(8,128)(2,1)S(1)} %get-tuple-element.570), channel_id=1, source_target_pairs={{0,1},{1,2},{2,3},{3,4},{4,5},{5,6},{6,7},{8,9},{9,10},{10,11},{11... | collective-permute-start | bytes 73736 | tf_op jit(solution)/shard_map/while/body/eval_jaxpr/ppermute | solution.py:12
  62.3 7.1 %collective-permute-start.2 = (bf16[2,1,24,256]{3,2,1,0:T(8,128)(2,1)S(1)}, bf16[2,1,24,256]{3,2,1,0:T(8,128)(2,1)S(1)}, u32[]{:S(2)}, u32[]{:S(2)}) collective-permute-start(bf16[2,1,24,256]{3,2,1,0:T(8,128)(2,1)S(1)} %get-tuple-element.572), channel_id=1, source_target_pairs={{1,0},{2,1},{3,2},{4,3},{5,4},{6,5},{7,6},{9,8},{10,9},{11,10},{12... | collective-permute-start | bytes 73736 | tf_op jit(solution)/shard_map/while/body/eval_jaxpr/ppermute | solution.py:15
  72.4 7.1 %collective-permute-start.4 = (bf16[2,1,24,256]{3,2,1,0:T(8,128)(2,1)S(1)}, bf16[2,1,24,256]{3,2,1,0:T(8,128)(2,1)S(1)}, u32[]{:S(2)}, u32[]{:S(2)}) collective-permute-start(bf16[2,1,24,256]{3,2,1,0:T(8,128)(2,1)S(1)} %get-tuple-element.577), channel_id=1, source_target_pairs={{1,0},{2,1},{3,2},{4,3},{5,4},{6,5},{7,6},{9,8},{10,9},{11,10},{12... | collective-permute-start | bytes 73736 | tf_op jit(solution)/shard_map/while/body/eval_jaxpr/ppermute | solution.py:15
  82.5 7.1 %collective-permute-start.6 = (bf16[2,1,24,256]{3,2,1,0:T(8,128)(2,1)S(1)}, bf16[2,1,24,256]{3,2,1,0:T(8,128)(2,1)S(1)}, u32[]{:S(2)}, u32[]{:S(2)}) collective-permute-start(bf16[2,1,24,256]{3,2,1,0:T(8,128)(2,1)S(1)} %get-tuple-element.580), channel_id=1, source_target_pairs={{1,0},{2,1},{3,2},{4,3},{5,4},{6,5},{7,6},{9,8},{10,9},{11,10},{12... | collective-permute-start | bytes 73736 | tf_op jit(solution)/shard_map/while/body/eval_jaxpr/ppermute | solution.py:15
  97.9 8.2 %collective-permute-start = (bf16[2,1,24,256]{3,2,1,0:T(8,128)(2,1)S(1)}, bf16[2,1,24,256]{3,2,1,0:T(8,128)(2,1)S(1)}, u32[]{:S(2)}, u32[]{:S(2)}) collective-permute-start(bf16[2,1,24,256]{3,2,1,0:T(8,128)(2,1)S(1)} %get-tuple-element.569), channel_id=1, source_target_pairs={{1,0},{2,1},{3,2},{4,3},{5,4},{6,5},{7,6},{9,8},{10,9},{11,10},{12... | collective-permute-start | bytes 73736 | tf_op jit(solution)/shard_map/while/body/eval_jaxpr/ppermute | solution.py:15
  99.8 7.2 %collective-permute-start.1 = (bf16[2,1,24,256]{3,2,1,0:T(8,128)(2,1)S(1)}, bf16[2,1,24,256]{3,2,1,0:T(8,128)(2,1)S(1)}, u32[]{:S(2)}, u32[]{:S(2)}) collective-permute-start(bf16[2,1,24,256]{3,2,1,0:T(8,128)(2,1)S(1)} %get-tuple-element.570), channel_id=1, source_target_pairs={{0,1},{1,2},{2,3},{3,4},{4,5},{5,6},{6,7},{8,9},{9,10},{10,11},{11... | collective-permute-start | bytes 73736 | tf_op jit(solution)/shard_map/while/body/eval_jaxpr/ppermute | solution.py:12
  109.1 7.1 %collective-permute-start.2 = (bf16[2,1,24,256]{3,2,1,0:T(8,128)(2,1)S(1)}, bf16[2,1,24,256]{3,2,1,0:T(8,128)(2,1)S(1)}, u32[]{:S(2)}, u32[]{:S(2)}) collective-permute-start(bf16[2,1,24,256]{3,2,1,0:T(8,128)(2,1)S(1)} %get-tuple-element.572), channel_id=1, source_target_pairs={{1,0},{2,1},{3,2},{4,3},{5,4},{6,5},{7,6},{9,8},{10,9},{11,10},{12... | collective-permute-start | bytes 73736 | tf_op jit(solution)/shard_map/while/body/eval_jaxpr/ppermute | solution.py:15
  119.2 7.1 %collective-permute-start.4 = (bf16[2,1,24,256]{3,2,1,0:T(8,128)(2,1)S(1)}, bf16[2,1,24,256]{3,2,1,0:T(8,128)(2,1)S(1)}, u32[]{:S(2)}, u32[]{:S(2)}) collective-permute-start(bf16[2,1,24,256]{3,2,1,0:T(8,128)(2,1)S(1)} %get-tuple-element.577), channel_id=1, source_target_pairs={{1,0},{2,1},{3,2},{4,3},{5,4},{6,5},{7,6},{9,8},{10,9},{11,10},{12... | collective-permute-start | bytes 73736 | tf_op jit(solution)/shard_map/while/body/eval_jaxpr/ppermute | solution.py:15
  129.2 7.1 %collective-permute-start.6 = (bf16[2,1,24,256]{3,2,1,0:T(8,128)(2,1)S(1)}, bf16[2,1,24,256]{3,2,1,0:T(8,128)(2,1)S(1)}, u32[]{:S(2)}, u32[]{:S(2)}) collective-permute-start(bf16[2,1,24,256]{3,2,1,0:T(8,128)(2,1)S(1)} %get-tuple-element.580), channel_id=1, source_target_pairs={{1,0},{2,1},{3,2},{4,3},{5,4},{6,5},{7,6},{9,8},{10,9},{11,10},{12... | collective-permute-start | bytes 73736 | tf_op jit(solution)/shard_map/while/body/eval_jaxpr/ppermute | solution.py:15
  144.6 8.2 %collective-permute-start = (bf16[2,1,24,256]{3,2,1,0:T(8,128)(2,1)S(1)}, bf16[2,1,24,256]{3,2,1,0:T(8,128)(2,1)S(1)}, u32[]{:S(2)}, u32[]{:S(2)}) collective-permute-start(bf16[2,1,24,256]{3,2,1,0:T(8,128)(2,1)S(1)} %get-tuple-element.569), channel_id=1, source_target_pairs={{1,0},{2,1},{3,2},{4,3},{5,4},{6,5},{7,6},{9,8},{10,9},{11,10},{12... | collective-permute-start | bytes 73736 | tf_op jit(solution)/shard_map/while/body/eval_jaxpr/ppermute | solution.py:15
  146.5 7.2 %collective-permute-start.1 = (bf16[2,1,24,256]{3,2,1,0:T(8,128)(2,1)S(1)}, bf16[2,1,24,256]{3,2,1,0:T(8,128)(2,1)S(1)}, u32[]{:S(2)}, u32[]{:S(2)}) collective-permute-start(bf16[2,1,24,256]{3,2,1,0:T(8,128)(2,1)S(1)} %get-tuple-element.570), channel_id=1, source_target_pairs={{0,1},{1,2},{2,3},{3,4},{4,5},{5,6},{6,7},{8,9},{9,10},{10,11},{11... | collective-permute-start | bytes 73736 | tf_op jit(solution)/shard_map/while/body/eval_jaxpr/ppermute | solution.py:12
  155.8 7.1 %collective-permute-start.2 = (bf16[2,1,24,256]{3,2,1,0:T(8,128)(2,1)S(1)}, bf16[2,1,24,256]{3,2,1,0:T(8,128)(2,1)S(1)}, u32[]{:S(2)}, u32[]{:S(2)}) collective-permute-start(bf16[2,1,24,256]{3,2,1,0:T(8,128)(2,1)S(1)} %get-tuple-element.572), channel_id=1, source_target_pairs={{1,0},{2,1},{3,2},{4,3},{5,4},{6,5},{7,6},{9,8},{10,9},{11,10},{12... | collective-permute-start | bytes 73736 | tf_op jit(solution)/shard_map/while/body/eval_jaxpr/ppermute | solution.py:15
  165.9 7.1 %collective-permute-start.4 = (bf16[2,1,24,256]{3,2,1,0:T(8,128)(2,1)S(1)}, bf16[2,1,24,256]{3,2,1,0:T(8,128)(2,1)S(1)}, u32[]{:S(2)}, u32[]{:S(2)}) collective-permute-start(bf16[2,1,24,256]{3,2,1,0:T(8,128)(2,1)S(1)} %get-tuple-element.577), channel_id=1, source_target_pairs={{1,0},{2,1},{3,2},{4,3},{5,4},{6,5},{7,6},{9,8},{10,9},{11,10},{12... | collective-permute-start | bytes 73736 | tf_op jit(solution)/shard_map/while/body/eval_jaxpr/ppermute | solution.py:15
  175.9 7.1 %collective-permute-start.6 = (bf16[2,1,24,256]{3,2,1,0:T(8,128)(2,1)S(1)}, bf16[2,1,24,256]{3,2,1,0:T(8,128)(2,1)S(1)}, u32[]{:S(2)}, u32[]{:S(2)}) collective-permute-start(bf16[2,1,24,256]{3,2,1,0:T(8,128)(2,1)S(1)} %get-tuple-element.580), channel_id=1, source_target_pairs={{1,0},{2,1},{3,2},{4,3},{5,4},{6,5},{7,6},{9,8},{10,9},{11,10},{12... | collective-permute-start | bytes 73736 | tf_op jit(solution)/shard_map/while/body/eval_jaxpr/ppermute | solution.py:15
  191.3 8.2 %collective-permute-start = (bf16[2,1,24,256]{3,2,1,0:T(8,128)(2,1)S(1)}, bf16[2,1,24,256]{3,2,1,0:T(8,128)(2,1)S(1)}, u32[]{:S(2)}, u32[]{:S(2)}) collective-permute-start(bf16[2,1,24,256]{3,2,1,0:T(8,128)(2,1)S(1)} %get-tuple-element.569), channel_id=1, source_target_pairs={{1,0},{2,1},{3,2},{4,3},{5,4},{6,5},{7,6},{9,8},{10,9},{11,10},{12... | collective-permute-start | bytes 73736 | tf_op jit(solution)/shard_map/while/body/eval_jaxpr/ppermute | solution.py:15
  193.3 7.2 %collective-permute-start.1 = (bf16[2,1,24,256]{3,2,1,0:T(8,128)(2,1)S(1)}, bf16[2,1,24,256]{3,2,1,0:T(8,128)(2,1)S(1)}, u32[]{:S(2)}, u32[]{:S(2)}) collective-permute-start(bf16[2,1,24,256]{3,2,1,0:T(8,128)(2,1)S(1)} %get-tuple-element.570), channel_id=1, source_target_pairs={{0,1},{1,2},{2,3},{3,4},{4,5},{5,6},{6,7},{8,9},{9,10},{10,11},{11... | collective-permute-start | bytes 73736 | tf_op jit(solution)/shard_map/while/body/eval_jaxpr/ppermute | solution.py:12
  202.6 7.1 %collective-permute-start.2 = (bf16[2,1,24,256]{3,2,1,0:T(8,128)(2,1)S(1)}, bf16[2,1,24,256]{3,2,1,0:T(8,128)(2,1)S(1)}, u32[]{:S(2)}, u32[]{:S(2)}) collective-permute-start(bf16[2,1,24,256]{3,2,1,0:T(8,128)(2,1)S(1)} %get-tuple-element.572), channel_id=1, source_target_pairs={{1,0},{2,1},{3,2},{4,3},{5,4},{6,5},{7,6},{9,8},{10,9},{11,10},{12... | collective-permute-start | bytes 73736 | tf_op jit(solution)/shard_map/while/body/eval_jaxpr/ppermute | solution.py:15
  212.6 7.1 %collective-permute-start.4 = (bf16[2,1,24,256]{3,2,1,0:T(8,128)(2,1)S(1)}, bf16[2,1,24,256]{3,2,1,0:T(8,128)(2,1)S(1)}, u32[]{:S(2)}, u32[]{:S(2)}) collective-permute-start(bf16[2,1,24,256]{3,2,1,0:T(8,128)(2,1)S(1)} %get-tuple-element.577), channel_id=1, source_target_pairs={{1,0},{2,1},{3,2},{4,3},{5,4},{6,5},{7,6},{9,8},{10,9},{11,10},{12... | collective-permute-start | bytes 73736 | tf_op jit(solution)/shard_map/while/body/eval_jaxpr/ppermute | solution.py:15
  222.7 7.1 %collective-permute-start.6 = (bf16[2,1,24,256]{3,2,1,0:T(8,128)(2,1)S(1)}, bf16[2,1,24,256]{3,2,1,0:T(8,128)(2,1)S(1)}, u32[]{:S(2)}, u32[]{:S(2)}) collective-permute-start(bf16[2,1,24,256]{3,2,1,0:T(8,128)(2,1)S(1)} %get-tuple-element.580), channel_id=1, source_target_pairs={{1,0},{2,1},{3,2},{4,3},{5,4},{6,5},{7,6},{9,8},{10,9},{11,10},{12... | collective-permute-start | bytes 73736 | tf_op jit(solution)/shard_map/while/body/eval_jaxpr/ppermute | solution.py:15
  238.1 8.2 %collective-permute-start = (bf16[2,1,24,256]{3,2,1,0:T(8,128)(2,1)S(1)}, bf16[2,1,24,256]{3,2,1,0:T(8,128)(2,1)S(1)}, u32[]{:S(2)}, u32[]{:S(2)}) collective-permute-start(bf16[2,1,24,256]{3,2,1,0:T(8,128)(2,1)S(1)} %get-tuple-element.569), channel_id=1, source_target_pairs={{1,0},{2,1},{3,2},{4,3},{5,4},{6,5},{7,6},{9,8},{10,9},{11,10},{12... | collective-permute-start | bytes 73736 | tf_op jit(solution)/shard_map/while/body/eval_jaxpr/ppermute | solution.py:15
  240.0 7.2 %collective-permute-start.1 = (bf16[2,1,24,256]{3,2,1,0:T(8,128)(2,1)S(1)}, bf16[2,1,24,256]{3,2,1,0:T(8,128)(2,1)S(1)}, u32[]{:S(2)}, u32[]{:S(2)}) collective-permute-start(bf16[2,1,24,256]{3,2,1,0:T(8,128)(2,1)S(1)} %get-tuple-element.570), channel_id=1, source_target_pairs={{0,1},{1,2},{2,3},{3,4},{4,5},{5,6},{6,7},{8,9},{9,10},{10,11},{11... | collective-permute-start | bytes 73736 | tf_op jit(solution)/shard_map/while/body/eval_jaxpr/ppermute | solution.py:12
  249.3 7.1 %collective-permute-start.2 = (bf16[2,1,24,256]{3,2,1,0:T(8,128)(2,1)S(1)}, bf16[2,1,24,256]{3,2,1,0:T(8,128)(2,1)S(1)}, u32[]{:S(2)}, u32[]{:S(2)}) collective-permute-start(bf16[2,1,24,256]{3,2,1,0:T(8,128)(2,1)S(1)} %get-tuple-element.572), channel_id=1, source_target_pairs={{1,0},{2,1},{3,2},{4,3},{5,4},{6,5},{7,6},{9,8},{10,9},{11,10},{12... | collective-permute-start | bytes 73736 | tf_op jit(solution)/shard_map/while/body/eval_jaxpr/ppermute | solution.py:15
  259.4 7.1 %collective-permute-start.4 = (bf16[2,1,24,256]{3,2,1,0:T(8,128)(2,1)S(1)}, bf16[2,1,24,256]{3,2,1,0:T(8,128)(2,1)S(1)}, u32[]{:S(2)}, u32[]{:S(2)}) collective-permute-start(bf16[2,1,24,256]{3,2,1,0:T(8,128)(2,1)S(1)} %get-tuple-element.577), channel_id=1, source_target_pairs={{1,0},{2,1},{3,2},{4,3},{5,4},{6,5},{7,6},{9,8},{10,9},{11,10},{12... | collective-permute-start | bytes 73736 | tf_op jit(solution)/shard_map/while/body/eval_jaxpr/ppermute | solution.py:15
  269.4 7.1 %collective-permute-start.6 = (bf16[2,1,24,256]{3,2,1,0:T(8,128)(2,1)S(1)}, bf16[2,1,24,256]{3,2,1,0:T(8,128)(2,1)S(1)}, u32[]{:S(2)}, u32[]{:S(2)}) collective-permute-start(bf16[2,1,24,256]{3,2,1,0:T(8,128)(2,1)S(1)} %get-tuple-element.580), channel_id=1, source_target_pairs={{1,0},{2,1},{3,2},{4,3},{5,4},{6,5},{7,6},{9,8},{10,9},{11,10},{12... | collective-permute-start | bytes 73736 | tf_op jit(solution)/shard_map/while/body/eval_jaxpr/ppermute | solution.py:15
  284.8 8.2 %collective-permute-start = (bf16[2,1,24,256]{3,2,1,0:T(8,128)(2,1)S(1)}, bf16[2,1,24,256]{3,2,1,0:T(8,128)(2,1)S(1)}, u32[]{:S(2)}, u32[]{:S(2)}) collective-permute-start(bf16[2,1,24,256]{3,2,1,0:T(8,128)(2,1)S(1)} %get-tuple-element.569), channel_id=1, source_target_pairs={{1,0},{2,1},{3,2},{4,3},{5,4},{6,5},{7,6},{9,8},{10,9},{11,10},{12... | collective-permute-start | bytes 73736 | tf_op jit(solution)/shard_map/while/body/eval_jaxpr/ppermute | solution.py:15
  286.8 7.2 %collective-permute-start.1 = (bf16[2,1,24,256]{3,2,1,0:T(8,128)(2,1)S(1)}, bf16[2,1,24,256]{3,2,1,0:T(8,128)(2,1)S(1)}, u32[]{:S(2)}, u32[]{:S(2)}) collective-permute-start(bf16[2,1,24,256]{3,2,1,0:T(8,128)(2,1)S(1)} %get-tuple-element.570), channel_id=1, source_target_pairs={{0,1},{1,2},{2,3},{3,4},{4,5},{5,6},{6,7},{8,9},{9,10},{10,11},{11... | collective-permute-start | bytes 73736 | tf_op jit(solution)/shard_map/while/body/eval_jaxpr/ppermute | solution.py:12
  296.0 7.1 %collective-permute-start.2 = (bf16[2,1,24,256]{3,2,1,0:T(8,128)(2,1)S(1)}, bf16[2,1,24,256]{3,2,1,0:T(8,128)(2,1)S(1)}, u32[]{:S(2)}, u32[]{:S(2)}) collective-permute-start(bf16[2,1,24,256]{3,2,1,0:T(8,128)(2,1)S(1)} %get-tuple-element.572), channel_id=1, source_target_pairs={{1,0},{2,1},{3,2},{4,3},{5,4},{6,5},{7,6},{9,8},{10,9},{11,10},{12... | collective-permute-start | bytes 73736 | tf_op jit(solution)/shard_map/while/body/eval_jaxpr/ppermute | solution.py:15
  316.2 7.1 %collective-permute-start.6 = (bf16[2,1,24,256]{3,2,1,0:T(8,128)(2,1)S(1)}, bf16[2,1,24,256]{3,2,1,0:T(8,128)(2,1)S(1)}, u32[]{:S(2)}, u32[]{:S(2)}) collective-permute-start(bf16[2,1,24,256]{3,2,1,0:T(8,128)(2,1)S(1)} %get-tuple-element.580), channel_id=1, source_target_pairs={{1,0},{2,1},{3,2},{4,3},{5,4},{6,5},{7,6},{9,8},{10,9},{11,10},{12... | collective-permute-start | bytes 73736 | tf_op jit(solution)/shard_map/while/body/eval_jaxpr/ppermute | solution.py:15
  (60 other events, 270.0 us)
where the time goes:
time: 337 us; the launch traced here: 331 us
  starting transfers between devices  213 us (63%)
  waiting for transfers between devices  53.7 us (16%)
  matrix products  26.7 us (8%)
  local copies, waits for them, and re-layouts  20.1 us (6%)
  other arithmetic  13 us (4%)
  loops' own time  4.45 us (1%)
    ppermute x28, starting transfers between devices, with_halo(): lax.ppermute(lax.slice_in_dim(block, block.shape[dim] - width, None, axis...  148 us
    ppermute x28, starting transfers between devices, with_halo(): lax.ppermute(lax.slice_in_dim(block, 0, width, axis=dim), axis, backward)  55.6 us
    ppermute x7, waiting for transfers between devices, from_behind(): lax.ppermute(value, axis, [(source, source + steps) for source in range(i...  28.4 us
    ppermute x28, waiting for transfers between devices, with_halo(): lax.ppermute(lax.slice_in_dim(block, block.shape[dim] - width, None, axis...  25.2 us
    while x217, local copies, waits for them, and re-layouts  15.5 us
    dot_general x28, matrix products, temporal_step(): jnp.dot(stacked.reshape(-1, stacked.shape[-1]), weight, preferred_element...  14.2 us
    dot_general x28, matrix products, tap_sum(): jnp.dot(stacked.reshape(-1, stacked.shape[-1]), kernel, preferred_element...  12.5 us
    ppermute x7, starting transfers between devices, from_behind(): lax.ppermute(value, axis, [(source, source + steps) for source in range(i...  9.04 us
  transfers between devices with their start and end apart: 63, of which 35 were waited for; matrix products, arithmetic and copies ran while one was open for 0% of the time, Pallas kernels for 0%

commit v1 on v0

v1 whole, which is shorter than its diff:
```python
import functools

import jax
import jax.numpy as jnp
from jax import lax
from jax.experimental import pallas as pl
from jax.experimental.pallas import tpu as pltpu
from jax.sharding import PartitionSpec as P

MESH = pl.DeviceIdType.MESH


def silu(v):
    half = 0.5 * v
    return half + half * jnp.tanh(half)


def edge_rows(v, width, low_ok, high_ok):
    low = jnp.where(low_ok, v[:width], 0.0)
    high = jnp.where(high_ok, v[-width:], 0.0)
    return jnp.concatenate([low, v[width:-width], high], 0)


def kernel(
    segments, spaces, rows, cols,
    depth_ref, video_ref, ws_hbm, wt_hbm, out_ref,
    own, left, right, ws, wt, even, odd, caches,
    w_sem, z_send, z_recv, l_send, l_recv, r_send, r_recv,
):
    frames, cells, channels = video_ref.shape
    place = lax.axis_index("segment")
    spot = lax.axis_index("space")
    has_left = spot > 0
    has_right = spot < spaces - 1
    has_prev = place > 0
    has_next = place < segments - 1

    def w_copies(i):
        return (
            pltpu.make_async_copy(ws_hbm.at[i], ws.at[i], w_sem.at[2 * i]),
            pltpu.make_async_copy(wt_hbm.at[i], wt.at[i], w_sem.at[2 * i + 1]),
        )

    for i in range(4):
        for c in w_copies(i):
            c.start()

    to_next = {"segment": place + 1}
    to_prev = {"segment": place - 1}
    to_left = {"space": spot - 1}
    to_right = {"space": spot + 1}
    partners = ((has_prev, to_prev), (has_next, to_next), (has_left, to_left), (has_right, to_right))

    barrier = pltpu.get_barrier_semaphore()
    for there, target in partners:
        @pl.when(there)
        def _():
            pl.semaphore_signal(barrier, inc=1, device_id=target, device_id_type=MESH)

    @pl.when(place == 0)
    def _():
        own[...] = video_ref[...]

    @pl.when(spot == 0)
    def _():
        left[...] = jnp.zeros_like(left)

    @pl.when(spot == spaces - 1)
    def _():
        right[...] = jnp.zeros_like(right)

    peers = sum(there.astype(jnp.int32) for there, _target in partners)
    pl.semaphore_wait(barrier, peers)

    def z_copy(f):
        return pltpu.make_async_remote_copy(
            out_ref.at[f], own.at[f], z_send.at[f], z_recv.at[f],
            device_id=to_next, device_id_type=MESH,
        )

    def l_copy(f):
        return pltpu.make_async_remote_copy(
            own.at[f], right.at[f], l_send.at[f], l_recv.at[f],
            device_id=to_left, device_id_type=MESH,
        )

    def r_copy(f):
        return pltpu.make_async_remote_copy(
            own.at[f], left.at[f], r_send.at[f], r_recv.at[f],
            device_id=to_right, device_id_type=MESH,
        )

    def forward(f):
        @pl.when(has_prev)
        def _():
            z_copy(f).wait_recv()

        @pl.when(has_left)
        def _():
            l_copy(f).start()

        @pl.when(has_right)
        def _():
            r_copy(f).start()

    def spread(v, stage):
        count = v.shape[0] // cols
        grid = v.reshape(count, cols, channels)
        column = lax.broadcasted_iota(jnp.int32, grid.shape, 1)
        before = pltpu.roll(v, 1, 0).reshape(grid.shape)
        after = pltpu.roll(v, v.shape[0] - 1, 0).reshape(grid.shape)
        taps = (
            jnp.where(column == 0, 0.0, before).reshape(v.shape),
            v,
            jnp.where(column == cols - 1, 0.0, after).reshape(v.shape),
        )
        inner = v.shape[0] - 2 * cols
        for c, tap in enumerate(taps):
            even[stage][c] = tap.astype(jnp.bfloat16)
            odd[stage][c] = tap[cols:cols + inner].astype(jnp.bfloat16)

    def spatial(stage):
        size = odd[stage].shape[1]
        pieces = (
            [even[stage][c, 0:size] for c in range(3)]
            + [odd[stage][c] for c in range(3)]
            + [even[stage][c, 2 * cols:2 * cols + size] for c in range(3)]
        )
        lhs = jnp.concatenate(pieces, -1)
        return jnp.dot(lhs, ws[stage], preferred_element_type=jnp.float32)

    def conv(f, stage):
        @pl.when(f == 0)
        def _():
            w_copies(stage)[0].wait()

        first = spatial(stage).astype(jnp.bfloat16)
        cache = caches[stage]
        cache[lax.rem(f, 3)] = first

        @pl.when(f == 0)
        def _():
            w_copies(stage)[1].wait()
            cache[1] = first
            cache[2] = first

        lhs = jnp.concatenate([cache[lax.rem(f + 1, 3)], cache[lax.rem(f + 2, 3)], first], -1)
        return jnp.dot(lhs, wt[stage], preferred_element_type=jnp.float32)

    deep = depth_ref[0] > 1
    forward(0)

    def tick(f, carry):
        @pl.when(has_left)
        def _():
            r_copy(f).wait_recv()

        @pl.when(has_right)
        def _():
            l_copy(f).wait_recv()

        x = jnp.concatenate([left[f], own[f], right[f]], 0).astype(jnp.float32)
        spread(silu(x), 0)
        b = edge_rows(silu(conv(f, 0)), 3 * cols, has_left, has_right)

        @pl.when(f + 1 < frames)
        def _():
            forward(f + 1)

        spread(b, 1)
        x1 = (x[2 * cols:-2 * cols] + conv(f, 1)).astype(jnp.bfloat16).astype(jnp.float32)
        x1 = edge_rows(x1, 2 * cols, has_left, has_right)
        spread(silu(x1), 2)
        b = edge_rows(silu(conv(f, 2)), cols, has_left, has_right)
        spread(b, 3)
        mid = x1[2 * cols:-2 * cols]
        x2 = mid + conv(f, 3)
        out_ref[f] = jnp.where(deep, x2, mid).astype(jnp.bfloat16)

        @pl.when(has_next)
        def _():
            z_copy(f).start()

        return carry

    lax.fori_loop(0, frames, tick, 0)

    def drain(f, carry):
        @pl.when(has_next)
        def _():
            z_copy(f).wait_send()

        @pl.when(has_left)
        def _():
            l_copy(f).wait_send()

        @pl.when(has_right)
        def _():
            r_copy(f).wait_send()

        return carry

    lax.fori_loop(0, frames, drain, 0)


def per_device(segments, spaces, video, spatial_weight, temporal_weight, section_blocks):
    micro, frames, rows, cols, channels = video.shape
    steps = micro * frames
    cells = rows * cols
    spatial_set = spatial_weight.reshape(4, 9 * channels, channels)
    temporal_set = temporal_weight.reshape(4, 3 * channels, channels)
    bf16 = jnp.bfloat16
    sizes = [(3 * rows - 2 * i) * cols for i in range(5)]
    dma = pltpu.SemaphoreType.DMA
    out = pl.pallas_call(
        functools.partial(kernel, segments, spaces, rows, cols),
        out_shape=jax.ShapeDtypeStruct((steps, cells, channels), bf16),
        in_specs=[
            pl.BlockSpec(memory_space=pltpu.SMEM),
            pl.BlockSpec(memory_space=pltpu.VMEM),
            pl.BlockSpec(memory_space=pl.ANY),
            pl.BlockSpec(memory_space=pl.ANY),
        ],
        out_specs=pl.BlockSpec(memory_space=pltpu.VMEM),
        scratch_shapes=[
            pltpu.VMEM((steps, cells, channels), bf16),
            pltpu.VMEM((steps, cells, channels), bf16),
            pltpu.VMEM((steps, cells, channels), bf16),
            pltpu.VMEM(spatial_set.shape, bf16),
            pltpu.VMEM(temporal_set.shape, bf16),
            [pltpu.VMEM((3, sizes[i], channels), bf16) for i in range(4)],
            [pltpu.VMEM((3, sizes[i + 1], channels), bf16) for i in range(4)],
            [pltpu.VMEM((3, sizes[i + 1], channels), bf16) for i in range(4)],
            dma((8,)),
            dma((steps,)), dma((steps,)), dma((steps,)),
            dma((steps,)), dma((steps,)), dma((steps,)),
        ],
        compiler_params=pltpu.CompilerParams(
            collective_id=0, has_side_effects=True, vmem_limit_bytes=48 * 2**20
        ),
        name="sections",
    )(section_blocks, video.reshape(steps, cells, channels), spatial_set, temporal_set)
    return out.reshape(1, micro, frames, rows, cols, channels)


def solution(mesh):
    return jax.shard_map(
        functools.partial(per_device, mesh.shape["segment"], mesh.shape["space"]),
        mesh=mesh,
        in_specs=(
            P(None, None, "space", None, None),
            P("segment", None, None, None, None),
            P("segment", None, None, None, None),
            P("segment"),
        ),
        out_specs=P("segment", None, None, "space", None, None),
        check_vma=False,
    )
```

time: 337 us -> 71.8 us (0.21); the launches traced: 331 us -> 71.7 us
  starting transfers between devices: 213 us -> 0 us
  Pallas kernels: 0 us -> 67.8 us
  waiting for transfers between devices: 53.7 us -> 0 us
  matrix products: 26.7 us -> 0 us
  local copies, waits for them, and re-layouts: 20.1 us -> 3.14 us
  other arithmetic: 13 us -> 0 us
  loops' own time: 4.45 us -> 0 us
    ppermute x63 -> x0, starting transfers between devices: 213 us -> none  [the longest x28 148 us: with_halo(): lax.ppermute(lax.slice_in_dim(block, block.shape[dim] - width, None, axis...]
    pallas_call x0 -> x1, Pallas kernels: none -> 67.8 us  [per_device(): pl.pallas_call(functools.partial(kernel, segments, spaces, rows, cols), o...]
    ppermute x63 -> x0, waiting for transfers between devices: 53.7 us -> none  [the longest x7 28.4 us: from_behind(): lax.ppermute(value, axis, [(source, source + steps) for source in range(i...]
    dot_general x56 -> x0, matrix products: 26.7 us -> none  [the longest x28 14.2 us: temporal_step(): jnp.dot(stacked.reshape(-1, stacked.shape[-1]), weight, preferred_element...]
    while x217 -> x0, local copies, waits for them, and re-layouts: 15.5 us -> none
    convert_element_type x7 -> x0, other arithmetic: 6.71 us -> none  [block_plain(): active = jax.nn.silu(state.astype(jnp.float32)).astype(jnp.bfloat16)]
    another operation x1 -> x0, loops' own time: 4.45 us -> none  [per_device(): lax.fori_loop(0, micro + segments - 1, advance, (incoming, caches, outputs))]
    concatenate x30 -> x0, other arithmetic: 3.64 us -> none  [the longest x28 1.89 us: with_halo(): block = jnp.concatenate([low, block, high], axis=dim)]
  transfers between devices with their start and end apart: 63 -> 0, of which waited for: 35 -> 0; matrix products, arithmetic and copies ran while one was open for 0% -> 0% of each run, Pallas kernels for 0% -> 0%
where the time goes in v1:
time: 71.8 us; the launch traced here: 71.7 us
  Pallas kernels  67.8 us (94%)
  local copies, waits for them, and re-layouts  3.14 us (4%)
    pallas_call x1, Pallas kernels, per_device(): pl.pallas_call(functools.partial(kernel, segments, spaces, rows, cols), o...  67.8 us
    unnamed x5, local copies, waits for them, and re-layouts  3.14 us

profile of v1, /device:TPU:27, one launch (start us, length us, event | category | flops | bytes accessed | tf_op | source)
XLA Modules:
  0.0 71.7 jit_solution(12145223783531727780)
XLA Ops:
  0.7 0.0 copy-start
  0.7 1.4 %copy-done = bf16[1,2,2,768,256]{4,3,2,1,0:T(8,128)(2,1)S(1)} copy-done((bf16[1,2,2,768,256]{4,3,2,1,0:T(8,128)(2,1)S(1)}, bf16[1,2,2,768,256]{4,3,2,1,0:T(8,128)(2,1)}, u32[]{:S(2)}) %copy-start) | copy-done | bytes 1572888
  2.1 0.0 copy-start.1
  2.1 1.0 %copy-done.1 = bf16[4,2,4,24,256]{4,3,2,1,0:T(8,128)(2,1)S(1)} copy-done((bf16[4,2,4,24,256]{4,3,2,1,0:T(8,128)(2,1)S(1)}, bf16[4,2,4,24,256]{4,3,2,1,0:T(8,128)(2,1)}, u32[]{:S(2)}) %copy-start.1) | copy-done | bytes 393240
  3.1 67.8 %sections.1 = bf16[8,96,256]{2,1,0:T(8,128)(2,1)S(1)} custom-call(s32[1]{0:T(128)S(6)} %copy.6.depth_ref, bf16[8,96,256]{2,1,0:T(8,128)(2,1)S(1)} %bitcast.6, bf16[4,2304,256]{2,1,0:T(8,128)(2,1)} %bitcast.7, bf16[4,768,256]{2,1,0:T(8,128)(2,1)S(1)} %bitcast.5), custom_call_target="tpu_custom_call" | custom-call | tf_op jit(solution)/shard_map/sections/pallas_call | solution.py:215
  70.9 0.7 %copy.7 = bf16[1,4,2,4,24,256]{5,4,3,2,1,0:T(8,128)(2,1)} copy(bf16[1,4,2,4,24,256]{5,4,3,2,1,0:T(8,128)(2,1)S(1)} %bitcast.4) | data formatting | bytes 786432
Async XLA Ops:
  0.7 1.4 %copy-start = (bf16[1,2,2,768,256]{4,3,2,1,0:T(8,128)(2,1)S(1)}, bf16[1,2,2,768,256]{4,3,2,1,0:T(8,128)(2,1)}, u32[]{:S(2)}) copy-start(bf16[1,2,2,768,256]{4,3,2,1,0:T(8,128)(2,1)} %param.6) | copy-start | bytes 4718596
  2.1 1.0 %copy-start.1 = (bf16[4,2,4,24,256]{4,3,2,1,0:T(8,128)(2,1)S(1)}, bf16[4,2,4,24,256]{4,3,2,1,0:T(8,128)(2,1)}, u32[]{:S(2)}) copy-start(bf16[4,2,4,24,256]{4,3,2,1,0:T(8,128)(2,1)} %param.4) | copy-start | bytes 1179652

commit v2 on v1

--- a/solution.py
+++ b/solution.py
@@ -121,36 +121,43 @@
 
     def spatial(stage):
         size = odd[stage].shape[1]
-        pieces = (
-            [even[stage][c, 0:size] for c in range(3)]
-            + [odd[stage][c] for c in range(3)]
-            + [even[stage][c, 2 * cols:2 * cols + size] for c in range(3)]
-        )
-        lhs = jnp.concatenate(pieces, -1)
-        return jnp.dot(lhs, ws[stage], preferred_element_type=jnp.float32)
-
-    def conv(f, stage):
-        @pl.when(f == 0)
-        def _():
+        lhs, rhs = [], []
+        for c in (1, 0, 2):
+            lhs += [even[stage][c, 0:size], odd[stage][c], even[stage][c, 2 * cols:2 * cols + size]]
+            rhs += [ws[stage, (3 * r + c) * channels:(3 * r + c + 1) * channels] for r in range(3)]
+        return jnp.dot(
+            jnp.concatenate(lhs, -1), jnp.concatenate(rhs, 0), preferred_element_type=jnp.float32
+        )
+
+    def conv(v, stage, first):
+        cache = caches[stage]
+        if first:
+            spread(v, stage)
             w_copies(stage)[0].wait()
-
-        first = spatial(stage).astype(jnp.bfloat16)
-        cache = caches[stage]
-        cache[lax.rem(f, 3)] = first
-
-        @pl.when(f == 0)
-        def _():
+            now = spatial(stage).astype(jnp.bfloat16)
             w_copies(stage)[1].wait()
-            cache[1] = first
-            cache[2] = first
-
-        lhs = jnp.concatenate([cache[lax.rem(f + 1, 3)], cache[lax.rem(f + 2, 3)], first], -1)
-        return jnp.dot(lhs, wt[stage], preferred_element_type=jnp.float32)
+            past = jnp.dot(
+                jnp.concatenate([now, now], -1), wt[stage, :2 * channels],
+                preferred_element_type=jnp.float32,
+            )
+            cache[0] = now
+            cache[1] = now
+        else:
+            older, newer = cache[0], cache[1]
+            past = jnp.dot(
+                jnp.concatenate([older, newer], -1), wt[stage, :2 * channels],
+                preferred_element_type=jnp.float32,
+            )
+            spread(v, stage)
+            now = spatial(stage).astype(jnp.bfloat16)
+            cache[0] = newer
+            cache[1] = now
+        return past + jnp.dot(now, wt[stage, 2 * channels:], preferred_element_type=jnp.float32)
 
     deep = depth_ref[0] > 1
     forward(0)
 
-    def tick(f, carry):
+    def tick(f, first):
         @pl.when(has_left)
         def _():
             r_copy(f).wait_recv()
@@ -160,30 +167,30 @@
             l_copy(f).wait_recv()
 
         x = jnp.concatenate([left[f], own[f], right[f]], 0).astype(jnp.float32)
-        spread(silu(x), 0)
-        b = edge_rows(silu(conv(f, 0)), 3 * cols, has_left, has_right)
+        b = edge_rows(silu(conv(silu(x), 0, first)), 3 * cols, has_left, has_right)
+        x1 = (x[2 * cols:-2 * cols] + conv(b, 1, first)).astype(jnp.bfloat16).astype(jnp.float32)
+        x1 = edge_rows(x1, 2 * cols, has_left, has_right)
 
         @pl.when(f + 1 < frames)
         def _():
             forward(f + 1)
 
-        spread(b, 1)
-        x1 = (x[2 * cols:-2 * cols] + conv(f, 1)).astype(jnp.bfloat16).astype(jnp.float32)
-        x1 = edge_rows(x1, 2 * cols, has_left, has_right)
-        spread(silu(x1), 2)
-        b = edge_rows(silu(conv(f, 2)), cols, has_left, has_right)
-        spread(b, 3)
+        b = edge_rows(silu(conv(silu(x1), 2, first)), cols, has_left, has_right)
         mid = x1[2 * cols:-2 * cols]
-        x2 = mid + conv(f, 3)
+        x2 = mid + conv(b, 3, first)
         out_ref[f] = jnp.where(deep, x2, mid).astype(jnp.bfloat16)
 
         @pl.when(has_next)
         def _():
             z_copy(f).start()
 
+    tick(0, True)
+
+    def later(f, carry):
+        tick(f, False)
         return carry
 
-    lax.fori_loop(0, frames, tick, 0)
+    lax.fori_loop(1, frames, later, 0)
 
     def drain(f, carry):
         @pl.when(has_next)
@@ -230,13 +237,13 @@
             pltpu.VMEM(temporal_set.shape, bf16),
             [pltpu.VMEM((3, sizes[i], channels), bf16) for i in range(4)],
             [pltpu.VMEM((3, sizes[i + 1], channels), bf16) for i in range(4)],
-            [pltpu.VMEM((3, sizes[i + 1], channels), bf16) for i in range(4)],
+            [pltpu.VMEM((2, sizes[i + 1], channels), bf16) for i in range(4)],
             dma((8,)),
             dma((steps,)), dma((steps,)), dma((steps,)),
             dma((steps,)), dma((steps,)), dma((steps,)),
         ],
         compiler_params=pltpu.CompilerParams(
-            collective_id=0, has_side_effects=True, vmem_limit_bytes=48 * 2**20
+            collective_id=0, has_side_effects=True, vmem_limit_bytes=60 * 2**20
         ),
         name="sections",
     )(section_blocks, video.reshape(steps, cells, channels), spatial_set, temporal_set)

time: 71.8 us -> 74.1 us (1.032)
  Pallas kernels: 67.8 us -> 71.4 us
  local copies, waits for them, and re-layouts: 3.14 us -> 1.77 us
    pallas_call x1, Pallas kernels: 67.8 us -> 71.4 us  [per_device(): pl.pallas_call(functools.partial(kernel, segments, spaces, rows, cols), o...]
    unnamed x5 -> x1, local copies, waits for them, and re-layouts: 3.14 us -> 1.77 us
where the time goes in v2:
time: 74.1 us; the launch traced here: 73.8 us
  Pallas kernels  71.4 us (96%)
  local copies, waits for them, and re-layouts  1.77 us (2%)
    pallas_call x1, Pallas kernels, per_device(): pl.pallas_call(functools.partial(kernel, segments, spaces, rows, cols), o...  71.4 us
    unnamed x1, local copies, waits for them, and re-layouts  1.77 us

profile of v2, /device:TPU:27, one launch (start us, length us, event | category | flops | bytes accessed | tf_op | source)
XLA Modules:
  0.0 73.8 jit_solution(3670924872782662782)
XLA Ops:
  0.7 71.4 %sections.1 = bf16[8,96,256]{2,1,0:T(8,128)(2,1)} custom-call(s32[1]{0:T(128)S(6)} %copy.6.depth_ref, bf16[8,96,256]{2,1,0:T(8,128)(2,1)} %bitcast.7, bf16[4,2304,256]{2,1,0:T(8,128)(2,1)} %bitcast.4, bf16[4,768,256]{2,1,0:T(8,128)(2,1)} %bitcast.6), custom_call_target="tpu_custom_call" | custom-call | tf_op jit(solution)/shard_map/sections/pallas_call | solution.py:222
  72.0 1.8 %copy.7 = bf16[1,4,2,4,24,256]{5,4,3,2,1,0:T(8,128)(2,1)} copy(bf16[1,4,2,4,24,256]{5,4,3,2,1,0:T(8,128)(2,1)} %bitcast.5) | data formatting | bytes 786432

commit v3 on v2

--- a/solution.py
+++ b/solution.py
@@ -24,7 +24,7 @@
 def kernel(
     segments, spaces, rows, cols,
     depth_ref, video_ref, ws_hbm, wt_hbm, out_ref,
-    own, left, right, ws, wt, even, odd, caches,
+    own, left, right, ws, wt, caches,
     w_sem, z_send, z_recv, l_send, l_recv, r_send, r_recv,
 ):
     frames, cells, channels = video_ref.shape
@@ -103,27 +103,22 @@
         def _():
             r_copy(f).start()
 
-    def spread(v, stage):
-        count = v.shape[0] // cols
-        grid = v.reshape(count, cols, channels)
-        column = lax.broadcasted_iota(jnp.int32, grid.shape, 1)
-        before = pltpu.roll(v, 1, 0).reshape(grid.shape)
-        after = pltpu.roll(v, v.shape[0] - 1, 0).reshape(grid.shape)
+    def spatial(v, stage):
+        grid = (v.shape[0] // cols, cols, channels)
+        size = v.shape[0] - 2 * cols
+        column = lax.broadcasted_iota(jnp.int32, grid, 1)
+        before = pltpu.roll(v, 1, 0).reshape(grid)
+        after = pltpu.roll(v, v.shape[0] - 1, 0).reshape(grid)
         taps = (
             jnp.where(column == 0, 0.0, before).reshape(v.shape),
             v,
             jnp.where(column == cols - 1, 0.0, after).reshape(v.shape),
         )
-        inner = v.shape[0] - 2 * cols
-        for c, tap in enumerate(taps):
-            even[stage][c] = tap.astype(jnp.bfloat16)
-            odd[stage][c] = tap[cols:cols + inner].astype(jnp.bfloat16)
-
-    def spatial(stage):
-        size = odd[stage].shape[1]
         lhs, rhs = [], []
         for c in (1, 0, 2):
-            lhs += [even[stage][c, 0:size], odd[stage][c], even[stage][c, 2 * cols:2 * cols + size]]
+            even = taps[c].astype(jnp.bfloat16)
+            odd = taps[c][cols:cols + size].astype(jnp.bfloat16)
+            lhs += [even[:size], odd, even[2 * cols:]]
             rhs += [ws[stage, (3 * r + c) * channels:(3 * r + c + 1) * channels] for r in range(3)]
         return jnp.dot(
             jnp.concatenate(lhs, -1), jnp.concatenate(rhs, 0), preferred_element_type=jnp.float32
@@ -131,28 +126,25 @@
 
     def conv(v, stage, first):
         cache = caches[stage]
+        wide = jnp.float32
         if first:
-            spread(v, stage)
             w_copies(stage)[0].wait()
-            now = spatial(stage).astype(jnp.bfloat16)
+            now = spatial(v, stage).astype(jnp.bfloat16)
             w_copies(stage)[1].wait()
             past = jnp.dot(
-                jnp.concatenate([now, now], -1), wt[stage, :2 * channels],
-                preferred_element_type=jnp.float32,
+                jnp.concatenate([now, now], -1), wt[stage, :2 * channels], preferred_element_type=wide
             )
-            cache[0] = now
-            cache[1] = now
+            cache[0] = now.astype(wide)
         else:
             older, newer = cache[0], cache[1]
             past = jnp.dot(
-                jnp.concatenate([older, newer], -1), wt[stage, :2 * channels],
-                preferred_element_type=jnp.float32,
+                jnp.concatenate([older, newer], -1).astype(jnp.bfloat16), wt[stage, :2 * channels],
+                preferred_element_type=wide,
             )
-            spread(v, stage)
-            now = spatial(stage).astype(jnp.bfloat16)
+            now = spatial(v, stage).astype(jnp.bfloat16)
             cache[0] = newer
-            cache[1] = now
-        return past + jnp.dot(now, wt[stage, 2 * channels:], preferred_element_type=jnp.float32)
+        cache[1] = now.astype(wide)
+        return past + jnp.dot(now, wt[stage, 2 * channels:], preferred_element_type=wide)
 
     deep = depth_ref[0] > 1
     forward(0)
@@ -235,9 +227,7 @@
             pltpu.VMEM((steps, cells, channels), bf16),
             pltpu.VMEM(spatial_set.shape, bf16),
             pltpu.VMEM(temporal_set.shape, bf16),
-            [pltpu.VMEM((3, sizes[i], channels), bf16) for i in range(4)],
-            [pltpu.VMEM((3, sizes[i + 1], channels), bf16) for i in range(4)],
-            [pltpu.VMEM((2, sizes[i + 1], channels), bf16) for i in range(4)],
+            [pltpu.VMEM((2, sizes[i + 1], channels), jnp.float32) for i in range(4)],
             dma((8,)),
             dma((steps,)), dma((steps,)), dma((steps,)),
             dma((steps,)), dma((steps,)), dma((steps,)),

time: 74.1 us -> 73.4 us (level)
  no operation moved by 1% of the time
where the time goes in v3:
time: 73.4 us; the launch traced here: 73.1 us
  Pallas kernels  70.7 us (96%)
  local copies, waits for them, and re-layouts  1.77 us (2%)
    pallas_call x1, Pallas kernels, per_device(): pl.pallas_call(functools.partial(kernel, segments, spaces, rows, cols), o...  70.7 us
    unnamed x1, local copies, waits for them, and re-layouts  1.77 us

profile of v3, /device:TPU:27, one launch (start us, length us, event | category | flops | bytes accessed | tf_op | source)
XLA Modules:
  0.0 73.1 jit_solution(10337225792728910360)
XLA Ops:
  0.7 70.7 %sections.1 = bf16[8,96,256]{2,1,0:T(8,128)(2,1)} custom-call(s32[1]{0:T(128)S(6)} %copy.6.depth_ref, bf16[8,96,256]{2,1,0:T(8,128)(2,1)} %bitcast.7, bf16[4,2304,256]{2,1,0:T(8,128)(2,1)} %bitcast.4, bf16[4,768,256]{2,1,0:T(8,128)(2,1)} %bitcast.6), custom_call_target="tpu_custom_call" | custom-call | tf_op jit(solution)/shard_map/sections/pallas_call | solution.py:214
  71.3 1.8 %copy.7 = bf16[1,4,2,4,24,256]{5,4,3,2,1,0:T(8,128)(2,1)} copy(bf16[1,4,2,4,24,256]{5,4,3,2,1,0:T(8,128)(2,1)} %bitcast.5) | data formatting | bytes 786432

commit v4 on v3

--- a/solution.py
+++ b/solution.py
@@ -8,6 +8,7 @@
 from jax.sharding import PartitionSpec as P
 
 MESH = pl.DeviceIdType.MESH
+GROUP = 2
 
 
 def silu(v):
@@ -27,7 +28,10 @@
     own, left, right, ws, wt, caches,
     w_sem, z_send, z_recv, l_send, l_recv, r_send, r_recv,
 ):
-    frames, cells, channels = video_ref.shape
+    ticks = video_ref.shape[0]
+    cells = rows * cols
+    group = video_ref.shape[1] // cells
+    channels = video_ref.shape[2]
     place = lax.axis_index("segment")
     spot = lax.axis_index("space")
     has_left = spot > 0
@@ -90,63 +94,74 @@
             device_id=to_right, device_id_type=MESH,
         )
 
+    def start_halo(f):
+        @pl.when(has_left)
+        def _():
+            l_copy(f).start()
+
+        @pl.when(has_right)
+        def _():
+            r_copy(f).start()
+
     def forward(f):
         @pl.when(has_prev)
         def _():
             z_copy(f).wait_recv()
-
-        @pl.when(has_left)
-        def _():
-            l_copy(f).start()
-
-        @pl.when(has_right)
-        def _():
-            r_copy(f).start()
-
-    def spatial(v, stage):
+            start_halo(f)
+
+    def taps(v):
         grid = (v.shape[0] // cols, cols, channels)
         size = v.shape[0] - 2 * cols
         column = lax.broadcasted_iota(jnp.int32, grid, 1)
         before = pltpu.roll(v, 1, 0).reshape(grid)
         after = pltpu.roll(v, v.shape[0] - 1, 0).reshape(grid)
-        taps = (
+        shifted = (
             jnp.where(column == 0, 0.0, before).reshape(v.shape),
             v,
             jnp.where(column == cols - 1, 0.0, after).reshape(v.shape),
         )
-        lhs, rhs = [], []
+        pieces = []
         for c in (1, 0, 2):
-            even = taps[c].astype(jnp.bfloat16)
-            odd = taps[c][cols:cols + size].astype(jnp.bfloat16)
-            lhs += [even[:size], odd, even[2 * cols:]]
-            rhs += [ws[stage, (3 * r + c) * channels:(3 * r + c + 1) * channels] for r in range(3)]
-        return jnp.dot(
-            jnp.concatenate(lhs, -1), jnp.concatenate(rhs, 0), preferred_element_type=jnp.float32
-        )
-
-    def conv(v, stage, first):
+            even = shifted[c].astype(jnp.bfloat16)
+            odd = shifted[c][cols:cols + size].astype(jnp.bfloat16)
+            pieces += [even[:size], odd, even[2 * cols:]]
+        return jnp.concatenate(pieces, -1)
+
+    def conv(vs, stage, first):
         cache = caches[stage]
         wide = jnp.float32
+        size = vs[0].shape[0] - 2 * cols
         if first:
             w_copies(stage)[0].wait()
-            now = spatial(v, stage).astype(jnp.bfloat16)
+        lhs = jnp.concatenate([taps(v) for v in vs], 0)
+        rhs = jnp.concatenate(
+            [ws[stage, (3 * r + c) * channels:(3 * r + c + 1) * channels] for c in (1, 0, 2) for r in range(3)], 0
+        )
+        now = jnp.dot(lhs, rhs, preferred_element_type=wide).astype(jnp.bfloat16)
+        nows = [now[g * size:(g + 1) * size] for g in range(len(vs))]
+        if first:
             w_copies(stage)[1].wait()
-            past = jnp.dot(
-                jnp.concatenate([now, now], -1), wt[stage, :2 * channels], preferred_element_type=wide
-            )
-            cache[0] = now.astype(wide)
+            line = [nows[0], nows[0]] + nows
         else:
-            older, newer = cache[0], cache[1]
-            past = jnp.dot(
-                jnp.concatenate([older, newer], -1).astype(jnp.bfloat16), wt[stage, :2 * channels],
-                preferred_element_type=wide,
-            )
-            now = spatial(v, stage).astype(jnp.bfloat16)
-            cache[0] = newer
-        cache[1] = now.astype(wide)
-        return past + jnp.dot(now, wt[stage, 2 * channels:], preferred_element_type=wide)
+            line = [cache[0].astype(jnp.bfloat16), cache[1].astype(jnp.bfloat16)] + nows
+        cache[0] = line[-2].astype(wide)
+        cache[1] = line[-1].astype(wide)
+        lhs = jnp.concatenate(
+            [jnp.concatenate(line[g:g + 3], -1) for g in range(len(vs))], 0
+        )
+        mixed = jnp.dot(lhs, wt[stage], preferred_element_type=wide)
+        return [mixed[g * size:(g + 1) * size] for g in range(len(vs))]
 
     deep = depth_ref[0] > 1
+
+    @pl.when(place == 0)
+    def _():
+        def send(f, carry):
+            start_halo(f)
+            return carry
+
+        lax.fori_loop(0, ticks, send, 0)
+
     forward(0)
 
     def tick(f, first):
@@ -158,19 +173,24 @@
         def _():
             l_copy(f).wait_recv()
 
-        x = jnp.concatenate([left[f], own[f], right[f]], 0).astype(jnp.float32)
-        b = edge_rows(silu(conv(silu(x), 0, first)), 3 * cols, has_left, has_right)
-        x1 = (x[2 * cols:-2 * cols] + conv(b, 1, first)).astype(jnp.bfloat16).astype(jnp.float32)
-        x1 = edge_rows(x1, 2 * cols, has_left, has_right)
-
-        @pl.when(f + 1 < frames)
+        xs = []
+        for g in range(group):
+            span = slice(g * cells, (g + 1) * cells)
+            xs.append(jnp.concatenate([left[f, span], own[f, span], right[f, span]], 0).astype(jnp.float32))
+        bs = [edge_rows(silu(q), 3 * cols, has_left, has_right) for q in conv([silu(x) for x in xs], 0, first)]
+        qs = conv(bs, 1, first)
+        x1s = [(x[2 * cols:-2 * cols] + q).astype(jnp.bfloat16).astype(jnp.float32) for x, q in zip(xs, qs)]
+        x1s = [edge_rows(x1, 2 * cols, has_left, has_right) for x1 in x1s]
+
+        @pl.when(f + 1 < ticks)
         def _():
             forward(f + 1)
 
-        b = edge_rows(silu(conv(silu(x1), 2, first)), cols, has_left, has_right)
-        mid = x1[2 * cols:-2 * cols]
-        x2 = mid + conv(b, 3, first)
-        out_ref[f] = jnp.where(deep, x2, mid).astype(jnp.bfloat16)
+        bs = [edge_rows(silu(q), cols, has_left, has_right) for q in conv([silu(x) for x in x1s], 2, first)]
+        qs = conv(bs, 3, first)
+        for g in range(group):
+            mid = x1s[g][2 * cols:-2 * cols]
+            out_ref[f, g * cells:(g + 1) * cells] = jnp.where(deep, mid + qs[g], mid).astype(jnp.bfloat16)
 
         @pl.when(has_next)
         def _():
@@ -182,7 +202,7 @@
         tick(f, False)
         return carry
 
-    lax.fori_loop(1, frames, later, 0)
+    lax.fori_loop(1, ticks, later, 0)
 
     def drain(f, carry):
         @pl.when(has_next)
@@ -199,13 +219,13 @@
 
         return carry
 
-    lax.fori_loop(0, frames, drain, 0)
+    lax.fori_loop(0, ticks, drain, 0)
 
 
 def per_device(segments, spaces, video, spatial_weight, temporal_weight, section_blocks):
     micro, frames, rows, cols, channels = video.shape
-    steps = micro * frames
-    cells = rows * cols
+    steps = micro * frames // GROUP
+    cells = GROUP * rows * cols
     spatial_set = spatial_weight.reshape(4, 9 * channels, channels)
     temporal_set = temporal_weight.reshape(4, 3 * channels, channels)
     bf16 = jnp.bfloat16

time: 73.4 us -> 72.1 us (0.982)
  Pallas kernels: 70.7 us -> 68.8 us
    pallas_call x1, Pallas kernels: 70.7 us -> 68.8 us  [per_device(): pl.pallas_call(functools.partial(kernel, segments, spaces, rows, cols), o...]
where the time goes in v4:
time: 72.1 us; the launch traced here: 71.3 us
  Pallas kernels  68.8 us (95%)
  local copies, waits for them, and re-layouts  1.77 us (2%)
    pallas_call x1, Pallas kernels, per_device(): pl.pallas_call(functools.partial(kernel, segments, spaces, rows, cols), o...  68.8 us
    unnamed x1, local copies, waits for them, and re-layouts  1.77 us

profile of v4, /device:TPU:27, one launch (start us, length us, event | category | flops | bytes accessed | tf_op | source)
XLA Modules:
  0.0 71.3 jit_solution(12231151697833015483)
XLA Ops:
  0.7 68.8 %sections.1 = bf16[4,192,256]{2,1,0:T(8,128)(2,1)} custom-call(s32[1]{0:T(128)S(6)} %copy.6.depth_ref, bf16[4,192,256]{2,1,0:T(8,128)(2,1)} %bitcast.7, bf16[4,2304,256]{2,1,0:T(8,128)(2,1)} %bitcast.4, bf16[4,768,256]{2,1,0:T(8,128)(2,1)} %bitcast.6), custom_call_target="tpu_custom_call" | custom-call | tf_op jit(solution)/shard_map/sections/pallas_call | solution.py:234
  69.5 1.8 %copy.7 = bf16[1,4,2,4,24,256]{5,4,3,2,1,0:T(8,128)(2,1)} copy(bf16[1,4,2,4,24,256]{5,4,3,2,1,0:T(8,128)(2,1)} %bitcast.5) | data formatting | bytes 786432

commit v5 on v4

--- a/solution.py
+++ b/solution.py
@@ -8,7 +8,7 @@
 from jax.sharding import PartitionSpec as P
 
 MESH = pl.DeviceIdType.MESH
-GROUP = 2
+GROUP = 1
 
 
 def silu(v):
@@ -25,7 +25,7 @@
 def kernel(
     segments, spaces, rows, cols,
     depth_ref, video_ref, ws_hbm, wt_hbm, out_ref,
-    own, left, right, ws, wt, caches,
+    own, left, right, ws_raw, wt_raw, ws, wt, caches,
     w_sem, z_send, z_recv, l_send, l_recv, r_send, r_recv,
 ):
     ticks = video_ref.shape[0]
@@ -41,8 +41,8 @@
 
     def w_copies(i):
         return (
-            pltpu.make_async_copy(ws_hbm.at[i], ws.at[i], w_sem.at[2 * i]),
-            pltpu.make_async_copy(wt_hbm.at[i], wt.at[i], w_sem.at[2 * i + 1]),
+            pltpu.make_async_copy(ws_hbm.at[i], ws_raw.at[i], w_sem.at[2 * i]),
+            pltpu.make_async_copy(wt_hbm.at[i], wt_raw.at[i], w_sem.at[2 * i + 1]),
         )
 
     for i in range(4):
@@ -133,14 +133,16 @@
         size = vs[0].shape[0] - 2 * cols
         if first:
             w_copies(stage)[0].wait()
+            ws[stage] = ws_raw[stage].astype(wide)
         lhs = jnp.concatenate([taps(v) for v in vs], 0)
         rhs = jnp.concatenate(
             [ws[stage, (3 * r + c) * channels:(3 * r + c + 1) * channels] for c in (1, 0, 2) for r in range(3)], 0
-        )
+        ).astype(jnp.bfloat16)
         now = jnp.dot(lhs, rhs, preferred_element_type=wide).astype(jnp.bfloat16)
         nows = [now[g * size:(g + 1) * size] for g in range(len(vs))]
         if first:
             w_copies(stage)[1].wait()
+            wt[stage] = wt_raw[stage].astype(wide)
             line = [nows[0], nows[0]] + nows
         else:
             line = [cache[0].astype(jnp.bfloat16), cache[1].astype(jnp.bfloat16)] + nows
@@ -149,7 +151,7 @@
         lhs = jnp.concatenate(
             [jnp.concatenate(line[g:g + 3], -1) for g in range(len(vs))], 0
         )
-        mixed = jnp.dot(lhs, wt[stage], preferred_element_type=wide)
+        mixed = jnp.dot(lhs, wt[stage].astype(jnp.bfloat16), preferred_element_type=wide)
         return [mixed[g * size:(g + 1) * size] for g in range(len(vs))]
 
     deep = depth_ref[0] > 1
@@ -178,13 +180,13 @@
             span = slice(g * cells, (g + 1) * cells)
             xs.append(jnp.concatenate([left[f, span], own[f, span], right[f, span]], 0).astype(jnp.float32))
         bs = [edge_rows(silu(q), 3 * cols, has_left, has_right) for q in conv([silu(x) for x in xs], 0, first)]
+        @pl.when(f + 1 < ticks)
+        def _():
+            forward(f + 1)
+
         qs = conv(bs, 1, first)
         x1s = [(x[2 * cols:-2 * cols] + q).astype(jnp.bfloat16).astype(jnp.float32) for x, q in zip(xs, qs)]
         x1s = [edge_rows(x1, 2 * cols, has_left, has_right) for x1 in x1s]
-
-        @pl.when(f + 1 < ticks)
-        def _():
-            forward(f + 1)
 
         bs = [edge_rows(silu(q), cols, has_left, has_right) for q in conv([silu(x) for x in x1s], 2, first)]
         qs = conv(bs, 3, first)
@@ -247,6 +249,8 @@
             pltpu.VMEM((steps, cells, channels), bf16),
             pltpu.VMEM(spatial_set.shape, bf16),
             pltpu.VMEM(temporal_set.shape, bf16),
+            pltpu.VMEM(spatial_set.shape, jnp.float32),
+            pltpu.VMEM(temporal_set.shape, jnp.float32),
             [pltpu.VMEM((2, sizes[i + 1], channels), jnp.float32) for i in range(4)],
             dma((8,)),
             dma((steps,)), dma((steps,)), dma((steps,)),

time: 72.1 us -> 67.1 us (0.931)
  Pallas kernels: 68.8 us -> 64.5 us
    pallas_call x1, Pallas kernels: 68.8 us -> 64.5 us  [per_device(): pl.pallas_call(functools.partial(kernel, segments, spaces, rows, cols), o...]
where the time goes in v5:
time: 67.1 us; the launch traced here: 66.9 us
  Pallas kernels  64.5 us (96%)
  local copies, waits for them, and re-layouts  1.77 us (3%)
    pallas_call x1, Pallas kernels, per_device(): pl.pallas_call(functools.partial(kernel, segments, spaces, rows, cols), o...  64.5 us
    unnamed x1, local copies, waits for them, and re-layouts  1.77 us

profile of v5, /device:TPU:27, one launch (start us, length us, event | category | flops | bytes accessed | tf_op | source)
XLA Modules:
  0.0 66.9 jit_solution(16878923739549861409)
XLA Ops:
  0.7 64.5 %sections.1 = bf16[8,96,256]{2,1,0:T(8,128)(2,1)} custom-call(s32[1]{0:T(128)S(6)} %copy.6.depth_ref, bf16[8,96,256]{2,1,0:T(8,128)(2,1)} %bitcast.7, bf16[4,2304,256]{2,1,0:T(8,128)(2,1)} %bitcast.4, bf16[4,768,256]{2,1,0:T(8,128)(2,1)} %bitcast.6), custom_call_target="tpu_custom_call" | custom-call | tf_op jit(solution)/shard_map/sections/pallas_call | solution.py:236
  65.1 1.8 %copy.7 = bf16[1,4,2,4,24,256]{5,4,3,2,1,0:T(8,128)(2,1)} copy(bf16[1,4,2,4,24,256]{5,4,3,2,1,0:T(8,128)(2,1)} %bitcast.5) | data formatting | bytes 786432

commit v6 on v5

--- a/solution.py
+++ b/solution.py
@@ -25,13 +25,14 @@
 def kernel(
     segments, spaces, rows, cols,
     depth_ref, video_ref, ws_hbm, wt_hbm, out_ref,
-    own, left, right, ws_raw, wt_raw, ws, wt, caches,
+    own, left, right, ws, wt, caches,
     w_sem, z_send, z_recv, l_send, l_recv, r_send, r_recv,
 ):
     ticks = video_ref.shape[0]
     cells = rows * cols
     group = video_ref.shape[1] // cells
     channels = video_ref.shape[2]
+    halves = channels // 128
     place = lax.axis_index("segment")
     spot = lax.axis_index("space")
     has_left = spot > 0
@@ -39,14 +40,17 @@
     has_prev = place > 0
     has_next = place < segments - 1
 
-    def w_copies(i):
-        return (
-            pltpu.make_async_copy(ws_hbm.at[i], ws_raw.at[i], w_sem.at[2 * i]),
-            pltpu.make_async_copy(wt_hbm.at[i], wt_raw.at[i], w_sem.at[2 * i + 1]),
-        )
+    def w_copies(i, which):
+        source, target = ((ws_hbm, ws), (wt_hbm, wt))[which]
+        return [
+            pltpu.make_async_copy(
+                source.at[i, :, pl.ds(128 * h, 128)], target.at[h, i], w_sem.at[(2 * i + which) * halves + h]
+            )
+            for h in range(halves)
+        ]
 
     for i in range(4):
-        for c in w_copies(i):
+        for c in w_copies(i, 0) + w_copies(i, 1):
             c.start()
 
     to_next = {"segment": place + 1}
@@ -107,7 +111,8 @@
         @pl.when(has_prev)
         def _():
             z_copy(f).wait_recv()
-            start_halo(f)
+
+        start_halo(f)
 
     def taps(v):
         grid = (v.shape[0] // cols, cols, channels)
@@ -132,17 +137,18 @@
         wide = jnp.float32
         size = vs[0].shape[0] - 2 * cols
         if first:
-            w_copies(stage)[0].wait()
-            ws[stage] = ws_raw[stage].astype(wide)
+            for c in w_copies(stage, 0):
+                c.wait()
         lhs = jnp.concatenate([taps(v) for v in vs], 0)
+        kernels = jnp.concatenate([ws[h, stage] for h in range(halves)], -1)
         rhs = jnp.concatenate(
-            [ws[stage, (3 * r + c) * channels:(3 * r + c + 1) * channels] for c in (1, 0, 2) for r in range(3)], 0
-        ).astype(jnp.bfloat16)
+            [kernels[(3 * r + c) * channels:(3 * r + c + 1) * channels] for c in (1, 0, 2) for r in range(3)], 0
+        )
         now = jnp.dot(lhs, rhs, preferred_element_type=wide).astype(jnp.bfloat16)
         nows = [now[g * size:(g + 1) * size] for g in range(len(vs))]
         if first:
-            w_copies(stage)[1].wait()
-            wt[stage] = wt_raw[stage].astype(wide)
+            for c in w_copies(stage, 1):
+                c.wait()
             line = [nows[0], nows[0]] + nows
         else:
             line = [cache[0].astype(jnp.bfloat16), cache[1].astype(jnp.bfloat16)] + nows
@@ -151,18 +157,11 @@
         lhs = jnp.concatenate(
             [jnp.concatenate(line[g:g + 3], -1) for g in range(len(vs))], 0
         )
-        mixed = jnp.dot(lhs, wt[stage].astype(jnp.bfloat16), preferred_element_type=wide)
+        kernels = jnp.concatenate([wt[h, stage] for h in range(halves)], -1)
+        mixed = jnp.dot(lhs, kernels, preferred_element_type=wide)
         return [mixed[g * size:(g + 1) * size] for g in range(len(vs))]
 
     deep = depth_ref[0] > 1
-
-    @pl.when(place == 0)
-    def _():
-        def send(f, carry):
-            start_halo(f)
-            return carry
-
-        lax.fori_loop(0, ticks, send, 0)
 
     forward(0)
 
@@ -247,12 +246,10 @@
             pltpu.VMEM((steps, cells, channels), bf16),
             pltpu.VMEM((steps, cells, channels), bf16),
             pltpu.VMEM((steps, cells, channels), bf16),
-            pltpu.VMEM(spatial_set.shape, bf16),
-            pltpu.VMEM(temporal_set.shape, bf16),
-            pltpu.VMEM(spatial_set.shape, jnp.float32),
-            pltpu.VMEM(temporal_set.shape, jnp.float32),
+            pltpu.VMEM((channels // 128, 4, 9 * channels, 128), bf16),
+            pltpu.VMEM((channels // 128, 4, 3 * channels, 128), bf16),
             [pltpu.VMEM((2, sizes[i + 1], channels), jnp.float32) for i in range(4)],
-            dma((8,)),
+            dma((8 * channels // 128,)),
             dma((steps,)), dma((steps,)), dma((steps,)),
             dma((steps,)), dma((steps,)), dma((steps,)),
         ],

time: 67.1 us -> 66.8 us (level)
  no operation moved by 1% of the time
where the time goes in v6:
time: 66.8 us; the launch traced here: 66.6 us
  Pallas kernels  64.2 us (96%)
  local copies, waits for them, and re-layouts  1.77 us (3%)
    pallas_call x1, Pallas kernels, per_device(): pl.pallas_call(functools.partial(kernel, segments, spaces, rows, cols), o...  64.2 us
    unnamed x1, local copies, waits for them, and re-layouts  1.77 us

profile of v6, /device:TPU:27, one launch (start us, length us, event | category | flops | bytes accessed | tf_op | source)
XLA Modules:
  0.0 66.6 jit_solution(10826360263562337813)
XLA Ops:
  0.7 64.2 %sections.1 = bf16[8,96,256]{2,1,0:T(8,128)(2,1)} custom-call(s32[1]{0:T(128)S(6)} %copy.6.depth_ref, bf16[8,96,256]{2,1,0:T(8,128)(2,1)} %bitcast.7, bf16[4,2304,256]{2,1,0:T(8,128)(2,1)} %bitcast.4, bf16[4,768,256]{2,1,0:T(8,128)(2,1)} %bitcast.6), custom_call_target="tpu_custom_call" | custom-call | tf_op jit(solution)/shard_map/sections/pallas_call | solution.py:235
  64.9 1.8 %copy.7 = bf16[1,4,2,4,24,256]{5,4,3,2,1,0:T(8,128)(2,1)} copy(bf16[1,4,2,4,24,256]{5,4,3,2,1,0:T(8,128)(2,1)} %bitcast.5) | data formatting | bytes 786432

commit v7 on v6

--- a/solution.py
+++ b/solution.py
@@ -166,6 +166,10 @@
     forward(0)
 
     def tick(f, first):
+        @pl.when(f + 1 < ticks)
+        def _():
+            forward(f + 1)
+
         @pl.when(has_left)
         def _():
             r_copy(f).wait_recv()
@@ -179,10 +183,6 @@
             span = slice(g * cells, (g + 1) * cells)
             xs.append(jnp.concatenate([left[f, span], own[f, span], right[f, span]], 0).astype(jnp.float32))
         bs = [edge_rows(silu(q), 3 * cols, has_left, has_right) for q in conv([silu(x) for x in xs], 0, first)]
-        @pl.when(f + 1 < ticks)
-        def _():
-            forward(f + 1)
-
         qs = conv(bs, 1, first)
         x1s = [(x[2 * cols:-2 * cols] + q).astype(jnp.bfloat16).astype(jnp.float32) for x, q in zip(xs, qs)]
         x1s = [edge_rows(x1, 2 * cols, has_left, has_right) for x1 in x1s]

time: 66.8 us -> 59.6 us (0.89)
  Pallas kernels: 64.2 us -> 57 us
    pallas_call x1, Pallas kernels: 64.2 us -> 57 us  [per_device(): pl.pallas_call(functools.partial(kernel, segments, spaces, rows, cols), o...]
where the time goes in v7:
time: 59.6 us; the launch traced here: 59.4 us
  Pallas kernels  57 us (96%)
  local copies, waits for them, and re-layouts  1.77 us (3%)
  between operations  0.66 us (1%)
    pallas_call x1, Pallas kernels, per_device(): pl.pallas_call(functools.partial(kernel, segments, spaces, rows, cols), o...  57 us
    unnamed x1, local copies, waits for them, and re-layouts  1.77 us

profile of v7, /device:TPU:27, one launch (start us, length us, event | category | flops | bytes accessed | tf_op | source)
XLA Modules:
  0.0 59.4 jit_solution(17452609478050208812)
XLA Ops:
  0.7 57.0 %sections.1 = bf16[8,96,256]{2,1,0:T(8,128)(2,1)} custom-call(s32[1]{0:T(128)S(6)} %copy.6.depth_ref, bf16[8,96,256]{2,1,0:T(8,128)(2,1)} %bitcast.7, bf16[4,2304,256]{2,1,0:T(8,128)(2,1)} %bitcast.4, bf16[4,768,256]{2,1,0:T(8,128)(2,1)} %bitcast.6), custom_call_target="tpu_custom_call" | custom-call | tf_op jit(solution)/shard_map/sections/pallas_call | solution.py:235
  57.6 1.8 %copy.7 = bf16[1,4,2,4,24,256]{5,4,3,2,1,0:T(8,128)(2,1)} copy(bf16[1,4,2,4,24,256]{5,4,3,2,1,0:T(8,128)(2,1)} %bitcast.5) | data formatting | bytes 786432

commit v8 on v7

--- a/solution.py
+++ b/solution.py
@@ -26,7 +26,7 @@
     segments, spaces, rows, cols,
     depth_ref, video_ref, ws_hbm, wt_hbm, out_ref,
     own, left, right, ws, wt, caches,
-    w_sem, z_send, z_recv, l_send, l_recv, r_send, r_recv,
+    v_sem, w_sem, z_send, z_recv, l_send, l_recv, r_send, r_recv,
 ):
     ticks = video_ref.shape[0]
     cells = rows * cols
@@ -49,10 +49,6 @@
             for h in range(halves)
         ]
 
-    for i in range(4):
-        for c in w_copies(i, 0) + w_copies(i, 1):
-            c.start()
-
     to_next = {"segment": place + 1}
     to_prev = {"segment": place - 1}
     to_left = {"space": spot - 1}
@@ -67,7 +63,13 @@
 
     @pl.when(place == 0)
     def _():
-        own[...] = video_ref[...]
+        fetch = pltpu.make_async_copy(video_ref, own, v_sem)
+        fetch.start()
+        fetch.wait()
+
+    for i in range(4):
+        for c in w_copies(i, 0) + w_copies(i, 1):
+            c.start()
 
     @pl.when(spot == 0)
     def _():
@@ -139,16 +141,30 @@
         if first:
             for c in w_copies(stage, 0):
                 c.wait()
+        early = not first and len(vs) == 1
+        if not first:
+            temporal = jnp.concatenate([wt[h, stage] for h in range(halves)], -1)
+        if early:
+            newer = cache[1]
+            past = jnp.dot(
+                jnp.concatenate([cache[0], newer], -1).astype(jnp.bfloat16), temporal[:2 * channels],
+                preferred_element_type=wide,
+            )
         lhs = jnp.concatenate([taps(v) for v in vs], 0)
         kernels = jnp.concatenate([ws[h, stage] for h in range(halves)], -1)
         rhs = jnp.concatenate(
             [kernels[(3 * r + c) * channels:(3 * r + c + 1) * channels] for c in (1, 0, 2) for r in range(3)], 0
         )
         now = jnp.dot(lhs, rhs, preferred_element_type=wide).astype(jnp.bfloat16)
+        if early:
+            cache[0] = newer
+            cache[1] = now.astype(wide)
+            return [past + jnp.dot(now, temporal[2 * channels:], preferred_element_type=wide)]
         nows = [now[g * size:(g + 1) * size] for g in range(len(vs))]
         if first:
             for c in w_copies(stage, 1):
                 c.wait()
+            temporal = jnp.concatenate([wt[h, stage] for h in range(halves)], -1)
             line = [nows[0], nows[0]] + nows
         else:
             line = [cache[0].astype(jnp.bfloat16), cache[1].astype(jnp.bfloat16)] + nows
@@ -157,8 +173,7 @@
         lhs = jnp.concatenate(
             [jnp.concatenate(line[g:g + 3], -1) for g in range(len(vs))], 0
         )
-        kernels = jnp.concatenate([wt[h, stage] for h in range(halves)], -1)
-        mixed = jnp.dot(lhs, kernels, preferred_element_type=wide)
+        mixed = jnp.dot(lhs, temporal, preferred_element_type=wide)
         return [mixed[g * size:(g + 1) * size] for g in range(len(vs))]
 
     deep = depth_ref[0] > 1
@@ -237,9 +252,9 @@
         out_shape=jax.ShapeDtypeStruct((steps, cells, channels), bf16),
         in_specs=[
             pl.BlockSpec(memory_space=pltpu.SMEM),
-            pl.BlockSpec(memory_space=pltpu.VMEM),
-            pl.BlockSpec(memory_space=pl.ANY),
-            pl.BlockSpec(memory_space=pl.ANY),
+            pl.BlockSpec(memory_space=pltpu.HBM),
+            pl.BlockSpec(memory_space=pltpu.HBM),
+            pl.BlockSpec(memory_space=pltpu.HBM),
         ],
         out_specs=pl.BlockSpec(memory_space=pltpu.VMEM),
         scratch_shapes=[
@@ -249,12 +264,13 @@
             pltpu.VMEM((channels // 128, 4, 9 * channels, 128), bf16),
             pltpu.VMEM((channels // 128, 4, 3 * channels, 128), bf16),
             [pltpu.VMEM((2, sizes[i + 1], channels), jnp.float32) for i in range(4)],
+            dma,
             dma((8 * channels // 128,)),
             dma((steps,)), dma((steps,)), dma((steps,)),
             dma((steps,)), dma((steps,)), dma((steps,)),
         ],
         compiler_params=pltpu.CompilerParams(
-            collective_id=0, has_side_effects=True, vmem_limit_bytes=60 * 2**20
+            collective_id=0, has_side_effects=True, vmem_limit_bytes=63 * 2**20
         ),
         name="sections",
     )(section_blocks, video.reshape(steps, cells, channels), spatial_set, temporal_set)

time: 59.6 us -> 60.5 us (1.015)
  Pallas kernels: 57 us -> 57.9 us
    pallas_call x1, Pallas kernels: 57 us -> 57.9 us  [per_device(): pl.pallas_call(functools.partial(kernel, segments, spaces, rows, cols), o...]
where the time goes in v8:
time: 60.5 us; the launch traced here: 60.3 us
  Pallas kernels  57.9 us (96%)
  local copies, waits for them, and re-layouts  1.77 us (3%)
  between operations  0.66 us (1%)
    pallas_call x1, Pallas kernels, per_device(): pl.pallas_call(functools.partial(kernel, segments, spaces, rows, cols), o...  57.9 us
    unnamed x1, local copies, waits for them, and re-layouts  1.77 us

profile of v8, /device:TPU:27, one launch (start us, length us, event | category | flops | bytes accessed | tf_op | source)
XLA Modules:
  0.0 60.3 jit_solution(2039897647408736875)
XLA Ops:
  0.7 57.9 %sections.1 = bf16[8,96,256]{2,1,0:T(8,128)(2,1)} custom-call(s32[1]{0:T(128)S(6)} %copy.6.depth_ref, bf16[8,96,256]{2,1,0:T(8,128)(2,1)} %bitcast.7, bf16[4,2304,256]{2,1,0:T(8,128)(2,1)} %bitcast.4, bf16[4,768,256]{2,1,0:T(8,128)(2,1)} %bitcast.6), custom_call_target="tpu_custom_call" | custom-call | tf_op jit(solution)/shard_map/sections/pallas_call | solution.py:250
  58.6 1.8 %copy.7 = bf16[1,4,2,4,24,256]{5,4,3,2,1,0:T(8,128)(2,1)} copy(bf16[1,4,2,4,24,256]{5,4,3,2,1,0:T(8,128)(2,1)} %bitcast.5) | data formatting | bytes 786432

commit v9 on v7

--- a/solution.py
+++ b/solution.py
@@ -115,15 +115,16 @@
         start_halo(f)
 
     def taps(v):
-        grid = (v.shape[0] // cols, cols, channels)
+        count = v.shape[0] // cols
         size = v.shape[0] - 2 * cols
-        column = lax.broadcasted_iota(jnp.int32, grid, 1)
-        before = pltpu.roll(v, 1, 0).reshape(grid)
-        after = pltpu.roll(v, v.shape[0] - 1, 0).reshape(grid)
+        last = cols - 8
+        sublane = lax.broadcasted_iota(jnp.int32, (count, 8, channels), 1)
+        before = pltpu.roll(v, 1, 0).reshape(count, cols, channels)
+        after = pltpu.roll(v, v.shape[0] - 1, 0).reshape(count, cols, channels)
         shifted = (
-            jnp.where(column == 0, 0.0, before).reshape(v.shape),
+            jnp.concatenate([jnp.where(sublane == 0, 0.0, before[:, :8]), before[:, 8:]], 1).reshape(v.shape),
             v,
-            jnp.where(column == cols - 1, 0.0, after).reshape(v.shape),
+            jnp.concatenate([after[:, :last], jnp.where(sublane == 7, 0.0, after[:, last:])], 1).reshape(v.shape),
         )
         pieces = []
         for c in (1, 0, 2):
@@ -151,9 +152,10 @@
                 c.wait()
             line = [nows[0], nows[0]] + nows
         else:
-            line = [cache[0].astype(jnp.bfloat16), cache[1].astype(jnp.bfloat16)] + nows
-        cache[0] = line[-2].astype(wide)
-        cache[1] = line[-1].astype(wide)
+            line = [jnp.concatenate([cache[i, h] for h in range(halves)], -1) for i in range(2)] + nows
+        for i in range(2):
+            for h in range(halves):
+                cache[i, h] = line[i - 2][:, 128 * h:128 * (h + 1)]
         lhs = jnp.concatenate(
             [jnp.concatenate(line[g:g + 3], -1) for g in range(len(vs))], 0
         )
@@ -248,7 +250,7 @@
             pltpu.VMEM((steps, cells, channels), bf16),
             pltpu.VMEM((channels // 128, 4, 9 * channels, 128), bf16),
             pltpu.VMEM((channels // 128, 4, 3 * channels, 128), bf16),
-            [pltpu.VMEM((2, sizes[i + 1], channels), jnp.float32) for i in range(4)],
+            [pltpu.VMEM((2, channels // 128, sizes[i + 1], 128), bf16) for i in range(4)],
             dma((8 * channels // 128,)),
             dma((steps,)), dma((steps,)), dma((steps,)),
             dma((steps,)), dma((steps,)), dma((steps,)),

time: 59.6 us -> 59.5 us (level)
  no operation moved by 1% of the time
where the time goes in v9:
time: 59.5 us; the launch traced here: 59.3 us
  Pallas kernels  56.9 us (96%)
  local copies, waits for them, and re-layouts  1.77 us (3%)
  between operations  0.66 us (1%)
    pallas_call x1, Pallas kernels, per_device(): pl.pallas_call(functools.partial(kernel, segments, spaces, rows, cols), o...  56.9 us
    unnamed x1, local copies, waits for them, and re-layouts  1.77 us

profile of v9, /device:TPU:27, one launch (start us, length us, event | category | flops | bytes accessed | tf_op | source)
XLA Modules:
  0.0 59.3 jit_solution(12584703043771743865)
XLA Ops:
  0.7 56.9 %sections.1 = bf16[8,96,256]{2,1,0:T(8,128)(2,1)} custom-call(s32[1]{0:T(128)S(6)} %copy.6.depth_ref, bf16[8,96,256]{2,1,0:T(8,128)(2,1)} %bitcast.7, bf16[4,2304,256]{2,1,0:T(8,128)(2,1)} %bitcast.4, bf16[4,768,256]{2,1,0:T(8,128)(2,1)} %bitcast.6), custom_call_target="tpu_custom_call" | custom-call | tf_op jit(solution)/shard_map/sections/pallas_call | solution.py:237
  57.5 1.8 %copy.7 = bf16[1,4,2,4,24,256]{5,4,3,2,1,0:T(8,128)(2,1)} copy(bf16[1,4,2,4,24,256]{5,4,3,2,1,0:T(8,128)(2,1)} %bitcast.5) | data formatting | bytes 786432

commit v10 on v9

--- a/solution.py
+++ b/solution.py
@@ -8,7 +8,7 @@
 from jax.sharding import PartitionSpec as P
 
 MESH = pl.DeviceIdType.MESH
-GROUP = 1
+GROUP = 2
 
 
 def silu(v):

time: 59.5 us -> 67.9 us (1.14)
  Pallas kernels: 56.9 us -> 65.1 us
    pallas_call x1, Pallas kernels: 56.9 us -> 65.1 us  [per_device(): pl.pallas_call(functools.partial(kernel, segments, spaces, rows, cols), o...]
where the time goes in v10:
time: 67.9 us; the launch traced here: 67.6 us
  Pallas kernels  65.1 us (96%)
  local copies, waits for them, and re-layouts  1.77 us (3%)
    pallas_call x1, Pallas kernels, per_device(): pl.pallas_call(functools.partial(kernel, segments, spaces, rows, cols), o...  65.1 us
    unnamed x1, local copies, waits for them, and re-layouts  1.77 us

profile of v10, /device:TPU:27, one launch (start us, length us, event | category | flops | bytes accessed | tf_op | source)
XLA Modules:
  0.0 67.6 jit_solution(17730385056876111216)
XLA Ops:
  0.7 65.1 %sections.1 = bf16[4,192,256]{2,1,0:T(8,128)(2,1)} custom-call(s32[1]{0:T(128)S(6)} %copy.6.depth_ref, bf16[4,192,256]{2,1,0:T(8,128)(2,1)} %bitcast.7, bf16[4,2304,256]{2,1,0:T(8,128)(2,1)} %bitcast.4, bf16[4,768,256]{2,1,0:T(8,128)(2,1)} %bitcast.6), custom_call_target="tpu_custom_call" | custom-call | tf_op jit(solution)/shard_map/sections/pallas_call | solution.py:237
  65.8 1.8 %copy.7 = bf16[1,4,2,4,24,256]{5,4,3,2,1,0:T(8,128)(2,1)} copy(bf16[1,4,2,4,24,256]{5,4,3,2,1,0:T(8,128)(2,1)} %bitcast.5) | data formatting | bytes 786432

commit v11 on v9

--- a/solution.py
+++ b/solution.py
@@ -20,6 +20,13 @@
     low = jnp.where(low_ok, v[:width], 0.0)
     high = jnp.where(high_ok, v[-width:], 0.0)
     return jnp.concatenate([low, v[width:-width], high], 0)
+
+
+def tall_dot(lhs, rhs):
+    rows = lhs.shape[0]
+    cut = (rows // 2 + 15) // 16 * 16
+    parts = [lhs] if rows <= 128 else [lhs[:cut], lhs[cut:]]
+    return jnp.concatenate([jnp.dot(p, rhs, preferred_element_type=jnp.float32) for p in parts], 0)
 
 
 def kernel(
@@ -135,7 +142,6 @@
 
     def conv(vs, stage, first):
         cache = caches[stage]
-        wide = jnp.float32
         size = vs[0].shape[0] - 2 * cols
         if first:
             for c in w_copies(stage, 0):
@@ -145,7 +151,7 @@
         rhs = jnp.concatenate(
             [kernels[(3 * r + c) * channels:(3 * r + c + 1) * channels] for c in (1, 0, 2) for r in range(3)], 0
         )
-        now = jnp.dot(lhs, rhs, preferred_element_type=wide).astype(jnp.bfloat16)
+        now = tall_dot(lhs, rhs).astype(jnp.bfloat16)
         nows = [now[g * size:(g + 1) * size] for g in range(len(vs))]
         if first:
             for c in w_copies(stage, 1):
@@ -160,7 +166,7 @@
             [jnp.concatenate(line[g:g + 3], -1) for g in range(len(vs))], 0
         )
         kernels = jnp.concatenate([wt[h, stage] for h in range(halves)], -1)
-        mixed = jnp.dot(lhs, kernels, preferred_element_type=wide)
+        mixed = tall_dot(lhs, kernels)
         return [mixed[g * size:(g + 1) * size] for g in range(len(vs))]
 
     deep = depth_ref[0] > 1

time: 59.5 us -> 58.1 us (0.976)
  Pallas kernels: 56.9 us -> 55.5 us
    pallas_call x1, Pallas kernels: 56.9 us -> 55.5 us  [per_device(): pl.pallas_call(functools.partial(kernel, segments, spaces, rows, cols), o...]
where the time goes in v11:
time: 58.1 us; the launch traced here: 58 us
  Pallas kernels  55.5 us (96%)
  local copies, waits for them, and re-layouts  1.77 us (3%)
  between operations  0.66 us (1%)
    pallas_call x1, Pallas kernels, per_device(): pl.pallas_call(functools.partial(kernel, segments, spaces, rows, cols), o...  55.5 us
    unnamed x1, local copies, waits for them, and re-layouts  1.77 us

profile of v11, /device:TPU:27, one launch (start us, length us, event | category | flops | bytes accessed | tf_op | source)
XLA Modules:
  0.0 58.0 jit_solution(13835885209046172286)
XLA Ops:
  0.7 55.5 %sections.1 = bf16[8,96,256]{2,1,0:T(8,128)(2,1)} custom-call(s32[1]{0:T(128)S(6)} %copy.6.depth_ref, bf16[8,96,256]{2,1,0:T(8,128)(2,1)} %bitcast.7, bf16[4,2304,256]{2,1,0:T(8,128)(2,1)} %bitcast.4, bf16[4,768,256]{2,1,0:T(8,128)(2,1)} %bitcast.6), custom_call_target="tpu_custom_call" | custom-call | tf_op jit(solution)/shard_map/sections/pallas_call | solution.py:243
  56.2 1.8 %copy.7 = bf16[1,4,2,4,24,256]{5,4,3,2,1,0:T(8,128)(2,1)} copy(bf16[1,4,2,4,24,256]{5,4,3,2,1,0:T(8,128)(2,1)} %bitcast.5) | data formatting | bytes 786432
